TPU v7x, 32 devices: a whole 2x2x4 slice. The times are simulated.
32 devices in a mesh: span: 8 (over y, x, core), space: 4 (over z).
Axes of the slice: x: 2, y: 2, z: 4, core: 2. Of those that a mesh axis runs over, the one named last changes fastest.
Arguments:
- latents: bfloat16 [96, 16, 3072], P('space', 'span'), may hold values from -6 to 6
- span_order: int32 [16], replicated, may hold values from 0 to 15, each once
- modulation: float32 [16, 6, 3072], P('span'), may hold values from -2 to 10
- qkv_weight: bfloat16 [3, 3072, 2048], P(None, None, 'space'), may hold values from -0.109375 to 0.109375
- out_weight: bfloat16 [2048, 3072], P('space'), may hold values from -0.125 to 0.125
- up_weight: bfloat16 [3072, 12288], P(None, 'space'), may hold values from -0.109375 to 0.109375
- down_weight: bfloat16 [12288, 3072], P('space'), may hold values from -0.0546875 to 0.0546875
Outputs:
- mixed: bfloat16 [96, 16, 3072], P('space', 'span')
Inputs may be any that keep to these rules, and one draw needn't show every extreme that they name: `span_order`: a permutation of the span places 0 to 15.
All inputs are finite; a program needn't handle non-finite values.
Results may differ from a plain program's by a relative error of at most 0.025.
The roundings to bfloat16 on the way count: a program that leaves them out, or rounds other values in their place, can miss the bound.
Values may be sent and summed in bfloat16 or wider, within the bound.
A program may use at most 192 MiB of HBM per device.

v0:
```python
import jax
import jax.numpy as jnp
from jax import lax
from jax.sharding import PartitionSpec as P

HD = 128


def norm_mod(rows, shift, scale):
    mean = jnp.mean(rows, axis=-1, keepdims=True)
    centred = rows - mean
    variance = jnp.mean(centred * centred, axis=-1, keepdims=True)
    return (centred * lax.rsqrt(variance + 1e-06) * (1.0 + scale) + shift).astype(jnp.bfloat16)


def body(latents, span_order, modulation, qkv_weight, out_weight, up_weight, down_weight):
    span_count = latents.shape[1]
    head_count = qkv_weight.shape[2] // HD
    my_start = lax.axis_index("span") * span_count
    my_places = lax.dynamic_slice_in_dim(span_order, my_start, span_count, 0)
    gathered = lax.all_gather(latents, "space", axis=0, tiled=True)
    group_rows = gathered.shape[0]
    gathered_f = gathered.astype(jnp.float32)
    normed = norm_mod(gathered_f, modulation[None, :, 0], modulation[None, :, 1])
    projected = jnp.einsum(
        "tcd,sdf->stcf", normed, qkv_weight, preferred_element_type=jnp.float32
    ).astype(jnp.bfloat16)
    query = projected[0].reshape(group_rows, span_count, head_count, HD)
    factor = 1.0 / HD**0.5
    running = jnp.full((head_count, span_count, group_rows), -1e30, jnp.float32)
    key_piece = lax.all_gather(projected[1], "span", axis=1, tiled=True)
    value_piece = lax.all_gather(projected[2], "span", axis=1, tiled=True)
    piece_spans = key_piece.shape[1]
    key_four = key_piece.reshape(group_rows, piece_spans, head_count, HD)
    value_four = value_piece.reshape(group_rows, piece_spans, head_count, HD)
    allowed = (span_order[None, :] <= my_places[:, None])[None, :, None, :, None]
    scores = (
        jnp.einsum("tahd,ubhd->hatbu", query, key_four, preferred_element_type=jnp.float32) * factor
    )
    scores = jnp.where(allowed, scores, -1e30)
    newest = jnp.maximum(running, jnp.max(scores, axis=(3, 4)))
    expo = jnp.where(allowed, jnp.exp(scores - newest[..., None, None]), 0.0)
    denom = jnp.sum(expo, axis=(3, 4))
    accum = jnp.einsum(
        "hatbu,ubhd->hatd",
        expo.astype(jnp.bfloat16),
        value_four,
        preferred_element_type=jnp.float32,
    )
    running, denom, accum = (newest, denom, accum)
    attended = (
        (accum / denom[..., None])
        .transpose(2, 1, 0, 3)
        .reshape(group_rows, span_count, head_count * HD)
        .astype(jnp.bfloat16)
    )
    rows = attended
    attn_sum = lax.psum_scatter(
        jnp.einsum("tck,kd->tcd", rows, out_weight, preferred_element_type=jnp.float32).astype(
            jnp.bfloat16
        ),
        "space",
        scatter_dimension=0,
        tiled=True,
    ).astype(jnp.float32)
    residual = (latents.astype(jnp.float32) + modulation[None, :, 2] * attn_sum).astype(
        jnp.bfloat16
    )
    second = norm_mod(
        lax.all_gather(residual, "space", axis=0, tiled=True).astype(jnp.float32),
        modulation[None, :, 3],
        modulation[None, :, 4],
    )
    hidden = jax.nn.gelu(
        jnp.einsum("tcd,df->tcf", second, up_weight, preferred_element_type=jnp.float32),
        approximate=True,
    ).astype(jnp.bfloat16)
    rows = hidden
    ffn_sum = lax.psum_scatter(
        jnp.einsum("tcf,fd->tcd", rows, down_weight, preferred_element_type=jnp.float32).astype(
            jnp.bfloat16
        ),
        "space",
        scatter_dimension=0,
        tiled=True,
    ).astype(jnp.float32)
    return (residual.astype(jnp.float32) + modulation[None, :, 5] * ffn_sum).astype(jnp.bfloat16)


def solution(mesh):
    return jax.shard_map(
        body,
        mesh=mesh,
        in_specs=(
            P("space", "span", None),
            P(),
            P("span", None, None),
            P(None, None, "space"),
            P("space", None),
            P(None, "space"),
            P("space", None),
        ),
        out_specs=P("space", "span", None),
        check_vma=False,
    )
```

profile of v0, /device:TPU:0, one launch (start us, length us, event | category | flops | bytes accessed | tf_op | source)
XLA Modules:
  0.0 239.9 jit_solution(8916185323109135952)
XLA Ops:
  6.5 0.7 all-gather.7.cloned.1.call-update
  7.3 1.7 slice_bitcast_fusion.1
  9.0 33.1 %all-gather.7.cloned.1.call-done = bf16[96,2,3072]{2,1,0:T(2,128)(2,1)} async-done(((bf16[24,2,3072]{2,1,0:T(2,128)(2,1)}), bf16[96,2,3072]{2,1,0:T(2,128)(2,1)}) %all-gather.7.cloned.1.call-update) | async-done | bytes 1179664 | tf_op jit(solution)/shard_map/all_gather | solution.py:21
  42.1 2.4 convert_reduce_fusion.1
  44.5 2.9 %fusion.23 = f32[96,2]{1,0:T(8,128)S(1)} fusion(bf16[96,2,3072]{2,1,0:T(2,128)(2,1)} %all-gather.7.cloned.1.call-done, f32[96,2]{1,0:T(8,128)S(1)} %broadcast_multiply_fusion), kind=kLoop, calls=%fused_computation.27 | loop fusion | flops 2359104 | bytes 1181184 | tf_op jit(solution)/shard_map/reduce_sum | solution.py:12
  47.5 2.5 %fusion.61 = bf16[96,2,3072,1]{2,1,0,3:T(2,128)(2,1)S(1)} fusion(bf16[96,2,3072]{2,1,0:T(2,128)(2,1)S(1)} %copy-done.2, f32[2,3072]{1,0:T(2,128)S(1)} %get-tuple-element.11, f32[2,3072]{1,0:T(2,128)S(1)} %get-tuple-element.12, f32[96,2]{1,0:T(8,128)S(1)} %add_rsqrt_fusion, f32[96,2]{1,0:T(8,128)S(1)} %broadcast_multiply_fusion), kind=kLoop, calls=%fused_computation.49 | loop fusion | flops 3538944 | bytes 2409984 | tf_op jit(solution)/shard_map/convert_element_type | solution.py:13
  50.0 5.7 %fusion.49 = bf16[3,96,2,512]{3,1,0,2:T(8,128)(2,1)S(1)} fusion(bf16[3,3072,512]{2,1,0:T(8,128)(2,1)} %param.10, bf16[96,2,3072,1]{2,1,0,3:T(2,128)(2,1)S(1)} %fusion.61), kind=kOutput, calls=%fused_computation.47 | convolution fusion | flops 1812234240 | bytes 11206656 | tf_op jit(solution)/shard_map/tcd,sdf->stcf/dot_general | solution.py:25
  55.7 0.8 fusion.97
  56.5 0.7 all-gather.13.cloned.1.call-update
  57.2 0.2 reduce-scatter.7.cloned.1.call-start
  57.5 0.1 dynamic_slice.3
  57.5 0.1 broadcast_compare_fusion
  57.7 23.8 %all-gather.11.cloned.1.call-done = bf16[1,96,16,512]{3,1,0,2:T(8,128)(2,1)} async-done(((bf16[1,96,2,512]{3,1,0,2:T(8,128)(2,1)}), bf16[1,96,16,512]{3,1,0,2:T(8,128)(2,1)}) %all-gather.11.cloned.1.call-update) | async-done | bytes 1572880 | tf_op jit(solution)/shard_map/all_gather | solution.py:31
  81.5 3.5 %reshape.102 = bf16[96,16,4,128]{3,2,0,1:T(4,128)(2,1)} reshape(bf16[1,96,16,512]{3,1,0,2:T(8,128)(2,1)} %all-gather.11.cloned.1.call-done) | data formatting | bytes 3145728 | tf_op jit(solution)/shard_map/reshape | solution.py:34
  85.0 3.4 %fusion.6 = (f32[4,2,96]{2,1,0:T(2,128)S(1)}, f32[4,96,16,96,2]{3,2,4,1,0:T(8,128)S(1)}) fusion(pred[2,16]{1,0:T(4,128)(4,1)S(1)} %broadcast_compare_fusion, bf16[96,2,4,128,1]{3,2,0,1,4:T(4,128)(2,1)S(1)} %bitcast.104, bf16[96,16,4,128,1]{3,2,0,1,4:T(4,128)(2,1)} %bitcast.100), kind=kOutput, calls=%fused_computation.8 | convolution fusion | flops 305528064 | bytes 6491168 | tf_op jit(solution)/shard_map/tahd,ubhd->hatbu/dot_general | solution.py:38
  88.4 3.6 %fusion.7 = (f32[4,2,96]{2,1,0:T(2,128)S(1)}, bf16[4,2,96,16,96]{2,3,1,4,0:T(8,128)(2,1)}) fusion(f32[4,96,16,96,2]{3,2,4,1,0:T(8,128)S(1)} %get-tuple-element.17, f32[4,2,96]{2,1,0:T(2,128)S(1)} %broadcast_maximum_fusion, pred[2,16]{1,0:T(4,128)(4,1)S(1)} %broadcast_compare_fusion), kind=kLoop, calls=%fused_computation.9 | loop fusion | flops 7077120 | bytes 7084064 | tf_op jit(solution)/shard_map/reduce_sum | solution.py:43
  92.1 17.0 %all-gather.13.cloned.1.call-done = bf16[1,96,16,512]{3,1,0,2:T(8,128)(2,1)} async-done(((bf16[1,96,2,512]{3,1,0,2:T(8,128)(2,1)}), bf16[1,96,16,512]{3,1,0,2:T(8,128)(2,1)}) %all-gather.13.cloned.1.call-update) | async-done | bytes 1572880 | tf_op jit(solution)/shard_map/all_gather | solution.py:32
  109.1 3.5 %reshape.103 = bf16[96,16,4,128]{3,2,0,1:T(4,128)(2,1)} reshape(bf16[1,96,16,512]{3,1,0,2:T(8,128)(2,1)} %all-gather.13.cloned.1.call-done) | data formatting | bytes 3145728 | tf_op jit(solution)/shard_map/reshape | solution.py:35
  112.6 4.4 %fusion.85 = bf16[4,2,12,8,128]{4,3,2,1,0:T(8,128)(2,1)S(1)} fusion(bf16[96,16,4,128,1]{3,2,0,1,4:T(4,128)(2,1)} %bitcast.101, bf16[4,2,96,16,96]{2,3,1,4,0:T(8,128)(2,1)} %get-tuple-element.6, f32[96,2,4]{0,1,2:T(2,128)S(1)} %bitcast.105), kind=kOutput, calls=%fused_computation.61 | convolution fusion | flops 302186496 | bytes 4131840 | tf_op jit(solution)/shard_map/hatbu,ubhd->hatd/dot_general | solution.py:44
  116.9 0.8 fusion.12
  117.8 1.1 copy.98
  119.0 29.3 %reduce-scatter.7.cloned.1.call-done = bf16[24,6144]{1,0:T(8,128)(2,1)} async-done(((bf16[96,6144]{1,0:T(8,128)(2,1)}), bf16[24,6144]{1,0:T(8,128)(2,1)}) %reduce-scatter.7.cloned.1.call-update) | async-done | bytes 294928
  148.3 1.8 add_convert_fusion.1
  150.0 0.3 reduce-scatter.9.cloned.1.call-start
  150.3 29.0 %all-gather.9.cloned.1.call-done = bf16[96,2,3072]{2,0,1:T(8,128)(2,1)} async-done(((bf16[24,2,3072]{2,0,1:T(8,128)(2,1)}), bf16[96,2,3072]{2,0,1:T(8,128)(2,1)}) %all-gather.9.cloned.1.call-update) | async-done | bytes 1179664 | tf_op jit(solution)/shard_map/all_gather | solution.py:70
  179.3 1.5 convert_reduce_fusion
  180.9 1.7 fusion.27
  182.6 17.4 %fusion.13 = bf16[2,12,8,3072]{3,2,1,0:T(8,128)(2,1)} fusion(bf16[3072,3072]{1,0:T(8,128)(2,1)} %param.13, bf16[3072,3072]{1,0:T(8,128)(2,1)} %param.12, bf16[96,2,3072]{2,0,1:T(8,128)(2,1)} %all-gather.9.cloned.1.call-done, f32[2,3072]{1,0:T(2,128)S(1)} %copy-done.7, f32[2,3072]{1,0:T(2,128)S(1)} %copy-done.8, f32[96,2]{0,1:T(2,128)S(1)} %add_rsqrt_fusion.1, ...), kind=kOutput, calls=%fused_computation.14 | convolution fusion | flops 7257194496 | bytes 40158720 | tf_op jit(solution)/shard_map/tcf,fd->tcd/dot_general | solution.py:80
  200.1 2.4 %copy.99 = bf16[2,12,8,3072]{3,2,0,1:T(8,128)(2,1)} copy(bf16[2,12,8,3072]{3,2,1,0:T(8,128)(2,1)} %fusion.13) | data formatting | bytes 2359296
  202.5 28.4 %reduce-scatter.9.cloned.1.call-done = bf16[24,6144]{1,0:T(8,128)(2,1)} async-done(((bf16[96,6144]{1,0:T(8,128)(2,1)}), bf16[24,6144]{1,0:T(8,128)(2,1)}) %reduce-scatter.9.cloned.1.call-update) | async-done | bytes 294928
  231.0 1.1 add_convert_fusion
  232.0 1.0 copy.73
  (34 shorter events, 0.3 us)
Async XLA Ops:
  6.5 110.4 %copy-start = (bf16[512,3072]{1,0:T(8,128)(2,1)S(1)}, bf16[512,3072]{1,0:T(8,128)(2,1)}, u32[]{:S(2)}) copy-start(bf16[512,3072]{1,0:T(8,128)(2,1)} %param.11) | copy-start | bytes 9437188
  6.5 35.6 %all-gather.7.cloned.1.call-start = ((), (), s32[]{:S(2)}) async-start(), calls=%async_computation.2 | async-start | bytes 1474560 | tf_op jit(solution)/shard_map/all_gather | solution.py:21
  7.3 74.2 %all-gather.11.cloned.1.call-start = ((), (), s32[]{:S(2)}) async-start(), calls=%async_computation.4 | async-start | bytes 1769472 | tf_op jit(solution)/shard_map/all_gather | solution.py:31
  42.1 5.3 %copy-start.2 = (bf16[96,2,3072]{2,1,0:T(2,128)(2,1)S(1)}, bf16[96,2,3072]{2,1,0:T(2,128)(2,1)}, u32[]{:S(2)}) copy-start(bf16[96,2,3072]{2,1,0:T(2,128)(2,1)} %all-gather.7.cloned.1.call-done) | copy-start | bytes 3538948
  50.0 7.5 %copy-start.9 = (s32[16]{0:T(128)S(1)}, s32[16]{0:T(128)}, u32[]{:S(2)}) copy-start(s32[16]{0:T(128)} %param.8) | copy-start | bytes 196
  56.5 52.6 %all-gather.13.cloned.1.call-start = ((), (), s32[]{:S(2)}) async-start(), calls=%async_computation.5 | async-start | bytes 1769472 | tf_op jit(solution)/shard_map/all_gather | solution.py:32
  57.2 91.0 %reduce-scatter.7.cloned.1.call-start = ((), (), s32[]{:S(2)}) async-start(), calls=%async_computation.6 | async-start | bytes 1474560
  117.7 30.5 %copy-start.4 = (bf16[24,2,3072]{2,1,0:T(2,128)(2,1)S(1)}, bf16[24,2,3072]{2,1,0:T(2,128)(2,1)}, u32[]{:S(2)}) copy-start(bf16[24,2,3072]{2,1,0:T(2,128)(2,1)} %param.7) | copy-start | bytes 884740
  117.8 30.5 %copy-start.6 = (f32[2,3072]{1,0:T(2,128)S(1)}, f32[2,3072]{1,0:T(2,128)}, u32[]{:S(2)}) copy-start(f32[2,3072]{1,0:T(2,128)} %get-tuple-element.13) | copy-start | bytes 73732
  118.9 63.7 %copy-start.7 = (f32[2,3072]{1,0:T(2,128)S(1)}, f32[2,3072]{1,0:T(2,128)}, u32[]{:S(2)}) copy-start(f32[2,3072]{1,0:T(2,128)} %get-tuple-element.14) | copy-start | bytes 73732
  118.9 63.7 %copy-start.8 = (f32[2,3072]{1,0:T(2,128)S(1)}, f32[2,3072]{1,0:T(2,128)}, u32[]{:S(2)}) copy-start(f32[2,3072]{1,0:T(2,128)} %get-tuple-element.15) | copy-start | bytes 73732
  118.9 60.4 %all-gather.9.cloned.1.call-start = ((), (), s32[]{:S(2)}) async-start(), calls=%async_computation.3 | async-start | bytes 1474560 | tf_op jit(solution)/shard_map/all_gather | solution.py:70
  150.0 80.9 %reduce-scatter.9.cloned.1.call-start = ((), (), s32[]{:S(2)}) async-start(), calls=%async_computation.7 | async-start | bytes 1474560
  182.6 50.4 %copy-start.1 = (bf16[512,3072]{1,0:T(8,128)(2,1)S(1)}, bf16[512,3072]{1,0:T(8,128)(2,1)}, u32[]{:S(2)}) copy-start(bf16[512,3072]{1,0:T(8,128)(2,1)} %param.11) | copy-start | bytes 9437188
  200.1 30.9 %copy-start.3 = (bf16[24,2,3072]{2,0,1:T(8,128)(2,1)S(1)}, bf16[24,2,3072]{2,0,1:T(8,128)(2,1)}, u32[]{:S(2)}) copy-start(bf16[24,2,3072]{2,0,1:T(8,128)(2,1)} %add_convert_fusion.1) | copy-start | bytes 884740
  200.1 30.9 %copy-start.5 = (f32[2,3072]{1,0:T(2,128)S(1)}, f32[2,3072]{1,0:T(2,128)}, u32[]{:S(2)}) copy-start(f32[2,3072]{1,0:T(2,128)} %get-tuple-element.10) | copy-start | bytes 73732
Sparse Core Ops, SparseCore 0:
  8.9 33.1 all-gather.6
  56.6 24.8 all-gather.10
  83.3 25.6 all-gather.12
  119.0 29.1 reduce-scatter.6
  150.2 29.1 all-gather.8
  202.6 28.2 reduce-scatter.8
where the time goes:
time: 240 us
  waiting for transfers between devices  162 us (68%)
  matrix products  31.7 us (13%)
  other arithmetic  19.3 us (8%)
  between operations  13.6 us (6%)
  local copies, waits for them, and re-layouts  12.5 us (5%)
    unnamed x8, waiting for transfers between devices  59.2 us
    all_gather x1, waiting for transfers between devices, body(): gathered = lax.all_gather(latents, 'space', axis=0, tiled=True)  33.1 us
    all_gather x1, waiting for transfers between devices, body(): lax.all_gather(residual, 'space', axis=0, tiled=True).astype(jnp.float32)  29 us
    all_gather x1, waiting for transfers between devices, body(): key_piece = lax.all_gather(projected[1], 'span', axis=1, tiled=True)  23.8 us
    dot_general x1, matrix products, body(): jnp.einsum('tcf,fd->tcd', rows, down_weight, preferred_element_type=jnp.f...  17.4 us
    all_gather x1, waiting for transfers between devices, body(): value_piece = lax.all_gather(projected[2], 'span', axis=1, tiled=True)  17 us
    dot_general x1, matrix products, body(): jnp.einsum('tcd,sdf->stcf', normed, qkv_weight, preferred_element_type=jn...  5.68 us
  transfers between devices with their start and end apart: 6, of which 6 were waited for; matrix products, arithmetic and copies ran while one was open for 5% of the time, Pallas kernels for 0%

commit v1 on v0

--- a/solution.py
+++ b/solution.py
@@ -1,9 +1,17 @@
+import functools
+
 import jax
 import jax.numpy as jnp
 from jax import lax
+from jax.experimental import pallas as pl
+from jax.experimental.pallas import tpu as pltpu
 from jax.sharding import PartitionSpec as P
 
 HD = 128
+CHUNKS = 4
+BLOCK = 512
+MESH = pl.DeviceIdType.MESH
+VMEM_BYTES = 62 * 1024 * 1024
 
 
 def norm_mod(rows, shift, scale):
@@ -13,7 +21,7 @@
     return (centred * lax.rsqrt(variance + 1e-06) * (1.0 + scale) + shift).astype(jnp.bfloat16)
 
 
-def body(latents, span_order, modulation, qkv_weight, out_weight, up_weight, down_weight):
+def plain_body(latents, span_order, modulation, qkv_weight, out_weight, up_weight, down_weight):
     span_count = latents.shape[1]
     head_count = qkv_weight.shape[2] // HD
     my_start = lax.axis_index("span") * span_count
@@ -87,9 +95,463 @@
     return (residual.astype(jnp.float32) + modulation[None, :, 5] * ffn_sum).astype(jnp.bfloat16)
 
 
+def flip(index, bit):
+    return index + bit * (1 - 2 * ((index // bit) % 2))
+
+
+def layer_kernel(
+    nz, ns, span_count, order_ref, key_order_ref, x_ref, mod_ref, qkv_hbm, out_hbm, up_hbm, down_hbm,
+    mixed_ref,
+    w_a, w_b, w_out, w_up, gathered, normed, query, kv, expo, scores, denom, attended, part,
+    from_left, from_right, from_left2, from_right2, resid, hidden, acc,
+    w_sem, ag_send, ag_recv, kv_send, kv_recv, rs_send, rs_recv,
+):
+    z = lax.axis_index("space")
+    me = lax.axis_index("span")
+    rows, width = x_ref.shape
+    tok = rows // span_count
+    wide = width // CHUNKS
+    last = nz - 1
+    heads = query.shape[1] // HD
+    down_blocks = width // BLOCK
+    first_blocks = w_b.shape[0]
+
+    def load(src, dst, slot):
+        return pltpu.make_async_copy(src, dst, w_sem.at[slot])
+
+    def columns(c, size):
+        return pl.ds(c * size, size)
+
+    qkv_loads = [load(qkv_hbm.at[i], w_a.at[i], i) for i in range(3)]
+    out_load = load(out_hbm, w_out, 3)
+    up_loads = [load(up_hbm.at[:, columns(i, BLOCK)], w_up.at[i], 4 + i) for i in range(w_up.shape[0])]
+    down_base = 4 + w_up.shape[0]
+    down_loads = [
+        load(
+            down_hbm.at[:, columns(i, BLOCK)],
+            w_b.at[i] if i < first_blocks else w_a.at[i - first_blocks],
+            down_base + i,
+        )
+        for i in range(down_blocks)
+    ]
+    for i in (1, 2, 0):
+        qkv_loads[i].start()
+
+    barrier = pltpu.get_barrier_semaphore()
+    for bit in (1, 2, 4):
+        pl.semaphore_signal(barrier, inc=1, device_id=(flip(me, bit), z), device_id_type=MESH)
+
+    @pl.when(z > 0)
+    def _():
+        pl.semaphore_signal(barrier, inc=1, device_id=(me, z - 1), device_id_type=MESH)
+
+    @pl.when(z < last)
+    def _():
+        pl.semaphore_signal(barrier, inc=1, device_id=(me, z + 1), device_id_type=MESH)
+
+    pl.semaphore_wait(barrier, 3 + jnp.where(z > 0, 1, 0) + jnp.where(z < last, 1, 0))
+
+    def ag_copy(which, way, s, c, src, dst):
+        return pltpu.make_async_remote_copy(
+            src_ref=src, dst_ref=dst,
+            send_sem=ag_send.at[which, way, s, c], recv_sem=ag_recv.at[which, way, s, c],
+            device_id=(me, z + 1 if way == 0 else z - 1), device_id_type=MESH,
+        )
+
+    def ag_sends(way, s):
+        return jnp.logical_and(z < last, z - s >= 0) if way == 0 else jnp.logical_and(z > 0, z + s <= last)
+
+    def ag_gets(way, s):
+        return z - 1 - s >= 0 if way == 0 else z + 1 + s <= last
+
+    def ag_own(which, own, buf, c):
+        for way in range(2):
+            @pl.when(ag_sends(way, 0))
+            def _():
+                ag_copy(which, way, 0, c, own.at[:, columns(c, wide)], buf.at[z, :, columns(c, wide)]).start()
+
+    def ag_step(which, buf, s, c):
+        for way in range(2):
+            block = z - 1 - s if way == 0 else z + 1 + s
+
+            @pl.when(ag_gets(way, s))
+            def _():
+                piece = buf.at[block, :, columns(c, wide)]
+                ag_copy(which, way, s, c, piece, piece).wait_recv()
+
+            if s + 1 < last:
+                @pl.when(ag_sends(way, s + 1))
+                def _():
+                    piece = buf.at[block, :, columns(c, wide)]
+                    ag_copy(which, way, s + 1, c, piece, piece).start()
+
+    def ag_drain(which, buf):
+        for way in range(2):
+            for s in range(last):
+                for c in range(CHUNKS):
+                    @pl.when(ag_sends(way, s))
+                    def _():
+                        piece = buf.at[0, :, columns(c, wide)]
+                        ag_copy(which, way, s, c, piece, piece).wait_send()
+
+    def norm_block(block, first):
+        r = block.astype(jnp.float32)
+        centred = r - jnp.mean(r, axis=-1, keepdims=True)
+        variance = jnp.mean(centred * centred, axis=-1, keepdims=True)
+        y = centred * lax.rsqrt(variance + 1e-06)
+        pieces = []
+        for a in range(span_count):
+            shift = mod_ref[a, first : first + 1, :]
+            scale = mod_ref[a, first + 1 : first + 2, :]
+            pieces.append(y[a * tok : (a + 1) * tok] * (1.0 + scale) + shift)
+        return jnp.concatenate(pieces, axis=0).astype(jnp.bfloat16)
+
+    for c in range(CHUNKS):
+        ag_own(0, x_ref, gathered, c)
+    out_load.start()
+    for copy in up_loads:
+        copy.start()
+    for copy in down_loads[:first_blocks]:
+        copy.start()
+    normed[z] = norm_block(x_ref[...], 0)
+    for s in range(last):
+        for c in range(CHUNKS):
+            ag_step(0, gathered, s, c)
+        for way in range(2):
+            @pl.when(ag_gets(way, s))
+            def _():
+                block = z - 1 - s if way == 0 else z + 1 + s
+                normed[block] = norm_block(gathered[block], 0)
+
+    def kv_copy(which, rel, bit):
+        piece = kv.at[which, flip_all(me, rel ^ bit)]
+        return pltpu.make_async_remote_copy(
+            src_ref=piece, dst_ref=piece,
+            send_sem=kv_send.at[which, rel], recv_sem=kv_recv.at[which, rel],
+            device_id=(flip(me, bit), z), device_id_type=MESH,
+        )
+
+    def flip_all(index, rel):
+        for bit in (1, 2, 4):
+            if rel & bit:
+                index = flip(index, bit)
+        return index
+
+    def kv_take(which, rel):
+        piece = kv.at[which, flip_all(me, rel)]
+        pltpu.make_async_remote_copy(
+            src_ref=piece, dst_ref=piece,
+            send_sem=kv_send.at[which, rel], recv_sem=kv_recv.at[which, rel],
+            device_id=(flip(me, 1), z), device_id_type=MESH,
+        ).wait_recv()
+
+    total_rows = nz * rows
+
+    def project(i):
+        qkv_loads[i].wait()
+        return jnp.dot(
+            normed[...].reshape(total_rows, width), w_a[i], preferred_element_type=jnp.float32
+        ).astype(jnp.bfloat16)
+
+    kv[0, me] = project(1)
+    kv_copy(0, 2, 2).start()
+    kv_copy(0, 4, 4).start()
+    kv_copy(0, 1, 1).start()
+    kv[1, me] = project(2)
+    kv_copy(1, 4, 4).start()
+    kv_copy(1, 2, 2).start()
+    kv_copy(1, 1, 1).start()
+    query[...] = project(0)
+    for copy in down_loads[first_blocks:]:
+        copy.start()
+    ag_drain(0, gathered)
+    kv_take(0, 2)
+    kv_copy(0, 6, 4).start()
+    kv_copy(0, 3, 1).start()
+    kv_take(0, 4)
+    kv_copy(0, 5, 1).start()
+    kv_take(1, 4)
+    kv_copy(1, 6, 2).start()
+    kv_copy(1, 5, 1).start()
+    kv_take(1, 2)
+    kv_copy(1, 3, 1).start()
+    kv_take(0, 6)
+    kv_copy(0, 7, 1).start()
+    for rel in (1, 3, 5, 7):
+        kv_take(0, rel)
+
+    keys_rows = ns * total_rows
+    factor = 1.0 / HD**0.5
+    places = [order_ref[me * span_count + a] for a in range(span_count)]
+
+    def head_scores(h):
+        lanes = pl.ds(pl.multiple_of(h * HD, HD), HD)
+        keys = kv[0, :, :, lanes].reshape(keys_rows, HD)
+        scores[...] = lax.dot_general(
+            query[:, lanes], keys, (((1,), (1,)), ((), ())), preferred_element_type=jnp.float32
+        )
+        key_order = key_order_ref[...]
+        for block in range(nz):
+            out = []
+            sums = []
+            for a in range(span_count):
+                at = block * rows + a * tok
+                allowed = key_order <= places[a]
+                sc = jnp.where(allowed, scores[at : at + tok, :] * factor, -1e30)
+                e = jnp.exp(sc - jnp.max(sc, axis=-1, keepdims=True))
+                e = jnp.where(allowed, e, 0.0)
+                out.append(e)
+                sums.append(jnp.broadcast_to(jnp.sum(e, axis=-1, keepdims=True), (tok, HD)))
+            expo[h, block * rows : (block + 1) * rows, :] = jnp.concatenate(out, axis=0).astype(jnp.bfloat16)
+            denom[h, block * rows : (block + 1) * rows, :] = jnp.concatenate(sums, axis=0)
+
+    half = heads // 2
+
+    @pl.loop(0, half)
+    def _(h):
+        head_scores(h)
+
+    kv_take(1, 6)
+    kv_copy(1, 7, 1).start()
+
+    @pl.loop(half, heads)
+    def _(h):
+        head_scores(h)
+
+    for rel in (1, 3, 5, 7):
+        kv_take(1, rel)
+
+    @pl.loop(0, heads)
+    def _(h):
+        lanes = pl.ds(pl.multiple_of(h * HD, HD), HD)
+        mixed_values = jnp.dot(
+            expo[h], kv[1, :, :, lanes].reshape(keys_rows, HD), preferred_element_type=jnp.float32
+        )
+        attended[:, lanes] = (mixed_values / denom[h]).astype(jnp.bfloat16)
+
+    for which in range(2):
+        for rel in range(1, 8):
+            kv_copy(which, rel, rel & -rel if rel != 6 else (4 if which == 0 else 2)).wait_send()
+
+    def rs_copy(which, way, s, c, owner):
+        buf = ((from_left, from_right), (from_left2, from_right2))[which][way]
+        return pltpu.make_async_remote_copy(
+            src_ref=part.at[owner, :, columns(c, wide)], dst_ref=buf.at[owner, :, columns(c, wide)],
+            send_sem=rs_send.at[which, way, s, c], recv_sem=rs_recv.at[which, way, s, c],
+            device_id=(me, z + 1 if way == 0 else z - 1), device_id_type=MESH,
+        )
+
+    def rs_start(which, c):
+        @pl.when(z == 0)
+        def _():
+            for s in range(last):
+                rs_copy(which, 0, s, c, last - s).start()
+
+        @pl.when(z == last)
+        def _():
+            for s in range(last):
+                rs_copy(which, 1, s, c, s).start()
+
+    def rs_pass(which, c):
+        for s in range(last):
+            for way in range(2):
+                owner = last - s if way == 0 else s
+                on = jnp.logical_and(z > 0, owner > z) if way == 0 else jnp.logical_and(z < last, owner < z)
+
+                @pl.when(on)
+                def _():
+                    copy = rs_copy(which, way, s, c, owner)
+                    copy.wait_recv()
+                    buf = ((from_left, from_right), (from_left2, from_right2))[which][way]
+                    at = columns(c, wide)
+                    part[owner, :, at] = (
+                        part[owner, :, at].astype(jnp.float32) + buf[owner, :, at].astype(jnp.float32)
+                    ).astype(jnp.bfloat16)
+                    copy.start()
+
+        acc[...] = part[z, :, columns(c, wide)].astype(jnp.float32)
+
+        @pl.when(z > 0)
+        def _():
+            rs_copy(which, 0, last - z, c, z).wait_recv()
+            buf = (from_left, from_left2)[which]
+            acc[...] += buf[z, :, columns(c, wide)].astype(jnp.float32)
+
+        @pl.when(z < last)
+        def _():
+            rs_copy(which, 1, z, c, z).wait_recv()
+            buf = (from_right, from_right2)[which]
+            acc[...] += buf[z, :, columns(c, wide)].astype(jnp.float32)
+
+    def rs_drain(which):
+        for s in range(last):
+            for way in range(2):
+                owner = last - s if way == 0 else s
+                for c in range(CHUNKS):
+                    @pl.when(owner > z if way == 0 else owner < z)
+                    def _():
+                        rs_copy(which, way, s, c, owner).wait_send()
+
+    def gated(base, gate, c):
+        pieces = []
+        for a in range(span_count):
+            span_rows = slice(a * tok, (a + 1) * tok)
+            factor_row = mod_ref[a, gate : gate + 1, columns(c, wide)]
+            pieces.append(base[span_rows] + factor_row * acc[span_rows, :])
+        return jnp.concatenate(pieces, axis=0).astype(jnp.bfloat16)
+
+    out_load.wait()
+    for c in range(CHUNKS):
+        part[:, :, columns(c, wide)] = (
+            jnp.dot(attended[...], w_out[:, columns(c, wide)], preferred_element_type=jnp.float32)
+            .astype(jnp.bfloat16)
+            .reshape(nz, rows, wide)
+        )
+        rs_start(0, c)
+    for c in range(CHUNKS + last - 1):
+        if c < CHUNKS:
+            at = columns(c, wide)
+            rs_pass(0, c)
+            resid[z, :, at] = gated(x_ref[:, at].astype(jnp.float32), 2, c)
+            ag_own(1, resid.at[z], resid, c)
+        for s in range(last - 1):
+            if 0 <= c - 1 - s < CHUNKS:
+                ag_step(1, resid, s, c - 1 - s)
+    rs_drain(0)
+    for c in range(CHUNKS):
+        ag_step(1, resid, last - 1, c)
+
+    @pl.loop(0, nz)
+    def _(block):
+        normed[block] = norm_block(resid[block], 3)
+
+    for copy in up_loads:
+        copy.wait()
+
+    @pl.loop(0, w_up.shape[0])
+    def _(i):
+        raised = jnp.dot(
+            normed[...].reshape(total_rows, width), w_up[i], preferred_element_type=jnp.float32
+        )
+        hidden[:, pl.ds(pl.multiple_of(i * BLOCK, BLOCK), BLOCK)] = jax.nn.gelu(
+            raised, approximate=True
+        ).astype(jnp.bfloat16)
+
+    ag_drain(1, resid)
+    done = 0
+    for i in range(down_blocks):
+        down_loads[i].wait()
+        weight = w_b[i] if i < first_blocks else w_a[i - first_blocks]
+        part[:, :, columns(i, BLOCK)] = (
+            jnp.dot(hidden[...], weight, preferred_element_type=jnp.float32)
+            .astype(jnp.bfloat16)
+            .reshape(nz, rows, BLOCK)
+        )
+        while done < CHUNKS and (done + 1) * wide <= (i + 1) * BLOCK:
+            rs_start(1, done)
+            done += 1
+    for c in range(CHUNKS):
+        at = columns(c, wide)
+        rs_pass(1, c)
+        mixed_ref[:, at] = gated(resid[z, :, at].astype(jnp.float32), 5, c)
+    rs_drain(1)
+
+
+def kernel_body(nz, ns, latents, span_order, modulation, qkv_weight, out_weight, up_weight, down_weight):
+    tok, span_count, width = latents.shape
+    rows = tok * span_count
+    total = rows * nz
+    head_cols = qkv_weight.shape[2]
+    heads = head_cols // HD
+    hid = up_weight.shape[1]
+    keys_rows = ns * total
+    x = latents.transpose(1, 0, 2).reshape(rows, width)
+    key_order = jnp.broadcast_to(
+        span_order.reshape(ns, 1, span_count, 1), (ns, nz, span_count, tok)
+    ).reshape(1, keys_rows)
+    blocks = width // BLOCK
+    later = qkv_weight.shape[0]
+    bf, f32 = jnp.bfloat16, jnp.float32
+    vmem = pl.BlockSpec(memory_space=pltpu.VMEM)
+    hbm = pl.BlockSpec(memory_space=pl.ANY)
+    grouped = pltpu.VMEM((nz, rows, width), bf)
+    flops = 2 * total * width * (4 * head_cols + 2 * hid) + 4 * total * keys_rows * head_cols
+    mixed = pl.pallas_call(
+        functools.partial(layer_kernel, nz, ns, span_count),
+        out_shape=jax.ShapeDtypeStruct((rows, width), bf),
+        in_specs=[pl.BlockSpec(memory_space=pltpu.SMEM), vmem, vmem, vmem, hbm, hbm, hbm, hbm],
+        out_specs=vmem,
+        scratch_shapes=[
+            pltpu.VMEM((later, width, head_cols), bf),
+            pltpu.VMEM((blocks - later, hid, BLOCK), bf),
+            pltpu.VMEM((head_cols, width), bf),
+            pltpu.VMEM((hid // BLOCK, width, BLOCK), bf),
+            grouped,
+            grouped,
+            pltpu.VMEM((total, head_cols), bf),
+            pltpu.VMEM((2, ns, total, head_cols), bf),
+            pltpu.VMEM((heads, total, keys_rows), bf),
+            pltpu.VMEM((total, keys_rows), f32),
+            pltpu.VMEM((heads, total, HD), f32),
+            pltpu.VMEM((total, head_cols), bf),
+            grouped,
+            grouped,
+            grouped,
+            grouped,
+            grouped,
+            grouped,
+            pltpu.VMEM((total, hid), bf),
+            pltpu.VMEM((rows, width // CHUNKS), f32),
+            pltpu.SemaphoreType.DMA((4 + hid // BLOCK + blocks,)),
+            pltpu.SemaphoreType.DMA((2, 2, nz - 1, CHUNKS)),
+            pltpu.SemaphoreType.DMA((2, 2, nz - 1, CHUNKS)),
+            pltpu.SemaphoreType.DMA((2, ns)),
+            pltpu.SemaphoreType.DMA((2, ns)),
+            pltpu.SemaphoreType.DMA((2, 2, nz - 1, CHUNKS)),
+            pltpu.SemaphoreType.DMA((2, 2, nz - 1, CHUNKS)),
+        ],
+        compiler_params=pltpu.CompilerParams(
+            collective_id=0, has_side_effects=True, vmem_limit_bytes=VMEM_BYTES
+        ),
+        cost_estimate=pl.CostEstimate(
+            flops=flops,
+            bytes_accessed=2 * width * (4 * head_cols + 2 * hid),
+            transcendentals=total * (keys_rows * heads + hid),
+        ),
+    )(span_order, key_order, x, modulation, qkv_weight, out_weight, up_weight, down_weight)
+    return mixed.reshape(span_count, tok, width).transpose(1, 0, 2)
+
+
+def fits(nz, ns, tok, span_count, width, head_cols, hid):
+    rows = tok * span_count
+    total = rows * nz
+    keys_rows = ns * total
+    weights = 2 * width * (4 * head_cols + 2 * hid) - 2 * width * 3 * head_cols
+    moving = 2 * (9 * total * width + 2 * (keys_rows + total) * head_cols)
+    moving += 2 * total * keys_rows * (head_cols // HD + 2) + 4 * total * head_cols
+    return (
+        ns == 8
+        and nz > 1
+        and rows % 16 == 0
+        and tok % 8 == 0
+        and head_cols == BLOCK
+        and width == hid
+        and width % BLOCK == 0
+        and width % (CHUNKS * HD) == 0
+        and weights + moving < VMEM_BYTES
+    )
+
+
+def body(nz, ns, latents, span_order, modulation, qkv_weight, out_weight, up_weight, down_weight):
+    args = (latents, span_order, modulation, qkv_weight, out_weight, up_weight, down_weight)
+    if fits(nz, ns, *latents.shape, qkv_weight.shape[2], up_weight.shape[1]):
+        return kernel_body(nz, ns, *args)
+    return plain_body(*args)
+
+
 def solution(mesh):
     return jax.shard_map(
-        body,
+        functools.partial(body, mesh.shape["space"], mesh.shape["span"]),
         mesh=mesh,
         in_specs=(
             P("space", "span", None),

time: 240 us -> 155 us (0.65)
  waiting for transfers between devices: 162 us -> 0 us
  Pallas kernels: 0 us -> 146 us
  matrix products: 31.7 us -> 0 us
  other arithmetic: 19.3 us -> 0 us
  between operations: 13.6 us -> 0.01 us
  local copies, waits for them, and re-layouts: 12.5 us -> 6.85 us
    pallas_call x0 -> x1, Pallas kernels: none -> 146 us  [kernel_body(): pl.pallas_call(functools.partial(layer_kernel, nz, ns, span_count), out_s...]
    all_gather x4 -> x0, waiting for transfers between devices: 103 us -> none  [the longest x1 33.1 us: body(): gathered = lax.all_gather(latents, 'space', axis=0, tiled=True)]
    unnamed x8 -> x0, waiting for transfers between devices: 59.2 us -> none
    dot_general x5 -> x0, matrix products: 31.7 us -> none  [the longest x1 17.4 us: body(): jnp.einsum('tcf,fd->tcd', rows, down_weight, preferred_element_type=jnp.f...]
    reduce_sum x5 -> x0, other arithmetic: 12.2 us -> none  [the longest x2 4.68 us: norm_mod(): variance = jnp.mean(centred * centred, axis=-1, keepdims=True)]
    convert_element_type x3 -> x0, other arithmetic: 5.31 us -> none  [the longest x1 2.5 us: norm_mod(): (centred * lax.rsqrt(variance + 1e-06) * (1.0 + scale) + shift).astype(jn...]
    reshape x2, local copies, waits for them, and re-layouts: 6.98 us -> 2.69 us  [the longest x1 1.98 us: kernel_body(): return mixed.reshape(span_count, tok, width).transpose(1, 0, 2)]
  transfers between devices with their start and end apart: 6 -> 0, of which waited for: 6 -> 0; matrix products, arithmetic and copies ran while one was open for 5% -> 0% of each run, Pallas kernels for 0% -> 0%
where the time goes in v1:
time: 155 us; the launch traced here: 153 us
  Pallas kernels  146 us (94%)
  local copies, waits for them, and re-layouts  6.85 us (4%)
    pallas_call x1, Pallas kernels, kernel_body(): pl.pallas_call(functools.partial(layer_kernel, nz, ns, span_count), out_s...  146 us

profile of v1, /device:TPU:0, one launch (start us, length us, event | category | flops | bytes accessed | tf_op | source)
XLA Modules:
  0.0 152.9 jit_solution(14056567046967746915)
XLA Ops:
  0.0 0.7 broadcast_in_dim.7
  0.7 0.1 broadcast_in_dim.8
  0.8 0.7 reshape.11.key_order_ref
  1.5 1.6 %copy.12.mod_ref = f32[2,6,3072]{2,1,0:T(8,128)} copy(f32[2,6,3072]{2,0,1:T(2,128)} %param.9) | data formatting | bytes 294912 | tf_op args[2]
  3.2 1.7 %copy.11 = bf16[2,24,3072]{2,1,0:T(8,128)(2,1)} copy(bf16[2,24,3072]{2,0,1:T(2,128)(2,1)} %bitcast.8) | data formatting | bytes 589824 | tf_op jit(solution)/shard_map/transpose | solution.py:468
  4.9 146.0 %shard_map.73 = bf16[48,3072]{1,0:T(8,128)(2,1)} custom-call(s32[16]{0:T(128)} %order_ref.1, s32[1,1536]{1,0:T(1,128)} %reshape.11.key_order_ref, bf16[48,3072]{1,0:T(8,128)(2,1)} %bitcast.7, f32[2,6,3072]{2,1,0:T(8,128)} %copy.12.mod_ref, bf16[3,3072,512]{2,1,0:T(8,128)(2,1)} %qkv_hbm.1, bf16[512,3072]{1,0:T(8,128)(2,1)} %out_hbm.1, ...), custom_call_target="tpu_custom_call" | custom-call | flops 10267656192 | bytes 50331648 | tf_op jit(solution)/shard_map/pallas_call | solution.py:479
  150.9 2.0 %copy.15 = bf16[2,24,3072]{2,0,1:T(2,128)(2,1)} copy(bf16[2,24,3072]{2,1,0:T(8,128)(2,1)} %bitcast.6) | data formatting | bytes 589824 | tf_op jit(solution)/shard_map/reshape | solution.py:522

commit v2 on v1

--- a/solution.py
+++ b/solution.py
@@ -2,6 +2,7 @@
 
 import jax
 import jax.numpy as jnp
+import numpy as np
 from jax import lax
 from jax.experimental import pallas as pl
 from jax.experimental.pallas import tpu as pltpu
@@ -100,10 +101,10 @@
 
 
 def layer_kernel(
-    nz, ns, span_count, order_ref, key_order_ref, x_ref, mod_ref, qkv_hbm, out_hbm, up_hbm, down_hbm,
+    nz, ns, span_count, order_ref, key_span_ref, latent_ref, mod_ref, qkv_hbm, out_hbm, up_hbm, down_hbm,
     mixed_ref,
-    w_a, w_b, w_out, w_up, gathered, normed, query, kv, expo, scores, denom, attended, part,
-    from_left, from_right, from_left2, from_right2, resid, hidden, acc,
+    x_ref, w_a, w_b, w_out, w_up, gathered, normed, query, kv, expo, scores, denom, attended, part,
+    from_left, from_right, from_left2, from_right2, resid, hidden, acc, key_order_ref,
     w_sem, ag_send, ag_recv, kv_send, kv_recv, rs_send, rs_recv,
 ):
     z = lax.axis_index("space")
@@ -112,7 +113,7 @@
     tok = rows // span_count
     wide = width // CHUNKS
     last = nz - 1
-    heads = query.shape[1] // HD
+    heads = query.shape[2] // HD
     down_blocks = width // BLOCK
     first_blocks = w_b.shape[0]
 
@@ -136,6 +137,8 @@
     ]
     for i in (1, 2, 0):
         qkv_loads[i].start()
+    stored = latent_ref[...].astype(jnp.float32)
+    x_ref[...] = jnp.concatenate([stored[:, a, :] for a in range(span_count)], axis=0).astype(jnp.bfloat16)
 
     barrier = pltpu.get_barrier_semaphore()
     for bit in (1, 2, 4):
@@ -201,10 +204,72 @@
         y = centred * lax.rsqrt(variance + 1e-06)
         pieces = []
         for a in range(span_count):
-            shift = mod_ref[a, first : first + 1, :]
-            scale = mod_ref[a, first + 1 : first + 2, :]
+            shift = mod_ref[first, a : a + 1, :]
+            scale = mod_ref[first + 1, a : a + 1, :]
             pieces.append(y[a * tok : (a + 1) * tok] * (1.0 + scale) + shift)
         return jnp.concatenate(pieces, axis=0).astype(jnp.bfloat16)
+
+    def flip_all(index, rel):
+        for bit in (1, 2, 4):
+            if rel & bit:
+                index = flip(index, bit)
+        return index
+
+    def kv_copy(which, rel, bit, block):
+        piece = kv.at[which, flip_all(me, rel ^ bit), block]
+        return pltpu.make_async_remote_copy(
+            src_ref=piece, dst_ref=piece,
+            send_sem=kv_send.at[which, rel, block], recv_sem=kv_recv.at[which, rel, block],
+            device_id=(flip(me, bit), z), device_id_type=MESH,
+        )
+
+    def kv_take(which, rel, block):
+        piece = kv.at[which, flip_all(me, rel), block]
+        pltpu.make_async_remote_copy(
+            src_ref=piece, dst_ref=piece,
+            send_sem=kv_send.at[which, rel, block], recv_sem=kv_recv.at[which, rel, block],
+            device_id=(flip(me, 1), z), device_id_type=MESH,
+        ).wait_recv()
+
+    def project(block, source, first):
+        rows_in = norm_block(source, 0)
+
+        def part_of(i):
+            if first:
+                qkv_loads[i].wait()
+            return jnp.dot(rows_in, w_a[i], preferred_element_type=jnp.float32).astype(jnp.bfloat16)
+
+        for which in range(2):
+            kv[which, me, block] = part_of(1 + which)
+            for bit in ((2, 4, 1), (4, 2, 1))[which]:
+                kv_copy(which, bit, bit, block).start()
+        query[block] = part_of(0)
+
+    def second_hop(block):
+        kv_take(0, 2, block)
+        kv_copy(0, 6, 4, block).start()
+        kv_copy(0, 3, 1, block).start()
+        kv_take(1, 4, block)
+        kv_copy(1, 6, 2, block).start()
+        kv_copy(1, 5, 1, block).start()
+        kv_take(0, 4, block)
+        kv_copy(0, 5, 1, block).start()
+        kv_take(1, 2, block)
+        kv_copy(1, 3, 1, block).start()
+
+    def third_hop(block):
+        for which in range(2):
+            kv_take(which, 6, block)
+            kv_copy(which, 7, 1, block).start()
+
+    def each_block(s, do):
+        if s == -1:
+            do(z)
+        elif s >= 0:
+            for way in range(2):
+                @pl.when(ag_gets(way, s))
+                def _():
+                    do(z - 1 - s if way == 0 else z + 1 + s)
 
     for c in range(CHUNKS):
         ag_own(0, x_ref, gathered, c)
@@ -213,84 +278,43 @@
         copy.start()
     for copy in down_loads[:first_blocks]:
         copy.start()
-    normed[z] = norm_block(x_ref[...], 0)
+    project(z, x_ref[...], True)
     for s in range(last):
         for c in range(CHUNKS):
             ag_step(0, gathered, s, c)
-        for way in range(2):
-            @pl.when(ag_gets(way, s))
-            def _():
-                block = z - 1 - s if way == 0 else z + 1 + s
-                normed[block] = norm_block(gathered[block], 0)
-
-    def kv_copy(which, rel, bit):
-        piece = kv.at[which, flip_all(me, rel ^ bit)]
-        return pltpu.make_async_remote_copy(
-            src_ref=piece, dst_ref=piece,
-            send_sem=kv_send.at[which, rel], recv_sem=kv_recv.at[which, rel],
-            device_id=(flip(me, bit), z), device_id_type=MESH,
-        )
-
-    def flip_all(index, rel):
-        for bit in (1, 2, 4):
-            if rel & bit:
-                index = flip(index, bit)
-        return index
-
-    def kv_take(which, rel):
-        piece = kv.at[which, flip_all(me, rel)]
-        pltpu.make_async_remote_copy(
-            src_ref=piece, dst_ref=piece,
-            send_sem=kv_send.at[which, rel], recv_sem=kv_recv.at[which, rel],
-            device_id=(flip(me, 1), z), device_id_type=MESH,
-        ).wait_recv()
-
-    total_rows = nz * rows
-
-    def project(i):
-        qkv_loads[i].wait()
-        return jnp.dot(
-            normed[...].reshape(total_rows, width), w_a[i], preferred_element_type=jnp.float32
-        ).astype(jnp.bfloat16)
-
-    kv[0, me] = project(1)
-    kv_copy(0, 2, 2).start()
-    kv_copy(0, 4, 4).start()
-    kv_copy(0, 1, 1).start()
-    kv[1, me] = project(2)
-    kv_copy(1, 4, 4).start()
-    kv_copy(1, 2, 2).start()
-    kv_copy(1, 1, 1).start()
-    query[...] = project(0)
+        each_block(s, lambda block: project(block, gathered[block], False))
+        each_block(s - 1, second_hop)
+        each_block(s - 2, third_hop)
     for copy in down_loads[first_blocks:]:
         copy.start()
+    each_block(last - 1, second_hop)
+    each_block(last - 2, third_hop)
+    each_block(last - 1, third_hop)
     ag_drain(0, gathered)
-    kv_take(0, 2)
-    kv_copy(0, 6, 4).start()
-    kv_copy(0, 3, 1).start()
-    kv_take(0, 4)
-    kv_copy(0, 5, 1).start()
-    kv_take(1, 4)
-    kv_copy(1, 6, 2).start()
-    kv_copy(1, 5, 1).start()
-    kv_take(1, 2)
-    kv_copy(1, 3, 1).start()
-    kv_take(0, 6)
-    kv_copy(0, 7, 1).start()
-    for rel in (1, 3, 5, 7):
-        kv_take(0, rel)
-
+
+    @pl.loop(0, nz)
+    def _(block):
+        for which in range(2):
+            for rel in (1, 3, 5, 7):
+                kv_take(which, rel, block)
+
+    total_rows = nz * rows
     keys_rows = ns * total_rows
     factor = 1.0 / HD**0.5
     places = [order_ref[me * span_count + a] for a in range(span_count)]
 
+    key_order = jnp.zeros((1, keys_rows), jnp.int32)
+    for span in range(ns * span_count):
+        key_order = jnp.where(key_span_ref[...] == span, order_ref[span], key_order)
+    key_order_ref[...] = key_order
+
     def head_scores(h):
+        key_order = key_order_ref[...]
         lanes = pl.ds(pl.multiple_of(h * HD, HD), HD)
-        keys = kv[0, :, :, lanes].reshape(keys_rows, HD)
+        keys = kv[0, :, :, :, lanes].reshape(keys_rows, HD)
         scores[...] = lax.dot_general(
-            query[:, lanes], keys, (((1,), (1,)), ((), ())), preferred_element_type=jnp.float32
-        )
-        key_order = key_order_ref[...]
+            query[:, :, lanes].reshape(total_rows, HD), keys, (((1,), (1,)), ((), ())), preferred_element_type=jnp.float32
+        )
         for block in range(nz):
             out = []
             sums = []
@@ -305,33 +329,24 @@
             expo[h, block * rows : (block + 1) * rows, :] = jnp.concatenate(out, axis=0).astype(jnp.bfloat16)
             denom[h, block * rows : (block + 1) * rows, :] = jnp.concatenate(sums, axis=0)
 
-    half = heads // 2
-
-    @pl.loop(0, half)
+    @pl.loop(0, heads)
     def _(h):
         head_scores(h)
-
-    kv_take(1, 6)
-    kv_copy(1, 7, 1).start()
-
-    @pl.loop(half, heads)
-    def _(h):
-        head_scores(h)
-
-    for rel in (1, 3, 5, 7):
-        kv_take(1, rel)
 
     @pl.loop(0, heads)
     def _(h):
         lanes = pl.ds(pl.multiple_of(h * HD, HD), HD)
         mixed_values = jnp.dot(
-            expo[h], kv[1, :, :, lanes].reshape(keys_rows, HD), preferred_element_type=jnp.float32
+            expo[h], kv[1, :, :, :, lanes].reshape(keys_rows, HD), preferred_element_type=jnp.float32
         )
         attended[:, lanes] = (mixed_values / denom[h]).astype(jnp.bfloat16)
 
-    for which in range(2):
-        for rel in range(1, 8):
-            kv_copy(which, rel, rel & -rel if rel != 6 else (4 if which == 0 else 2)).wait_send()
+    @pl.loop(0, nz)
+    def _(block):
+        for which in range(2):
+            for rel in range(1, 8):
+                bit = rel & -rel if rel != 6 else (4 if which == 0 else 2)
+                kv_copy(which, rel, bit, block).wait_send()
 
     def rs_copy(which, way, s, c, owner):
         buf = ((from_left, from_right), (from_left2, from_right2))[which][way]
@@ -396,7 +411,7 @@
         pieces = []
         for a in range(span_count):
             span_rows = slice(a * tok, (a + 1) * tok)
-            factor_row = mod_ref[a, gate : gate + 1, columns(c, wide)]
+            factor_row = mod_ref[gate, a : a + 1, columns(c, wide)]
             pieces.append(base[span_rows] + factor_row * acc[span_rows, :])
         return jnp.concatenate(pieces, axis=0).astype(jnp.bfloat16)
 
@@ -465,9 +480,8 @@
     heads = head_cols // HD
     hid = up_weight.shape[1]
     keys_rows = ns * total
-    x = latents.transpose(1, 0, 2).reshape(rows, width)
-    key_order = jnp.broadcast_to(
-        span_order.reshape(ns, 1, span_count, 1), (ns, nz, span_count, tok)
+    key_span = np.broadcast_to(
+        np.arange(ns * span_count, dtype=np.int32).reshape(ns, 1, span_count, 1), (ns, nz, span_count, tok)
     ).reshape(1, keys_rows)
     blocks = width // BLOCK
     later = qkv_weight.shape[0]
@@ -482,14 +496,15 @@
         in_specs=[pl.BlockSpec(memory_space=pltpu.SMEM), vmem, vmem, vmem, hbm, hbm, hbm, hbm],
         out_specs=vmem,
         scratch_shapes=[
+            pltpu.VMEM((rows, width), bf),
             pltpu.VMEM((later, width, head_cols), bf),
             pltpu.VMEM((blocks - later, hid, BLOCK), bf),
             pltpu.VMEM((head_cols, width), bf),
             pltpu.VMEM((hid // BLOCK, width, BLOCK), bf),
             grouped,
             grouped,
-            pltpu.VMEM((total, head_cols), bf),
-            pltpu.VMEM((2, ns, total, head_cols), bf),
+            pltpu.VMEM((nz, rows, head_cols), bf),
+            pltpu.VMEM((2, ns, nz, rows, head_cols), bf),
             pltpu.VMEM((heads, total, keys_rows), bf),
             pltpu.VMEM((total, keys_rows), f32),
             pltpu.VMEM((heads, total, HD), f32),
@@ -502,11 +517,12 @@
             grouped,
             pltpu.VMEM((total, hid), bf),
             pltpu.VMEM((rows, width // CHUNKS), f32),
+            pltpu.VMEM((1, keys_rows), jnp.int32),
             pltpu.SemaphoreType.DMA((4 + hid // BLOCK + blocks,)),
             pltpu.SemaphoreType.DMA((2, 2, nz - 1, CHUNKS)),
             pltpu.SemaphoreType.DMA((2, 2, nz - 1, CHUNKS)),
-            pltpu.SemaphoreType.DMA((2, ns)),
-            pltpu.SemaphoreType.DMA((2, ns)),
+            pltpu.SemaphoreType.DMA((2, ns, nz)),
+            pltpu.SemaphoreType.DMA((2, ns, nz)),
             pltpu.SemaphoreType.DMA((2, 2, nz - 1, CHUNKS)),
             pltpu.SemaphoreType.DMA((2, 2, nz - 1, CHUNKS)),
         ],
@@ -518,7 +534,7 @@
             bytes_accessed=2 * width * (4 * head_cols + 2 * hid),
             transcendentals=total * (keys_rows * heads + hid),
         ),
-    )(span_order, key_order, x, modulation, qkv_weight, out_weight, up_weight, down_weight)
+    )(span_order, key_span, latents, modulation.transpose(1, 0, 2), qkv_weight, out_weight, up_weight, down_weight)
     return mixed.reshape(span_count, tok, width).transpose(1, 0, 2)
 
 

time: 155 us -> 146 us (0.942); the launches traced: 153 us -> 146 us
  local copies, waits for them, and re-layouts: 6.85 us -> 1.98 us
  Pallas kernels: 146 us -> 144 us
    pallas_call x1, Pallas kernels: 146 us -> 144 us  [kernel_body(): pl.pallas_call(functools.partial(layer_kernel, nz, ns, span_count), out_s...]
    transpose x1 -> x0, local copies, waits for them, and re-layouts: 1.72 us -> none  [kernel_body(): x = latents.transpose(1, 0, 2).reshape(rows, width)]
    unnamed x1 -> x0, local copies, waits for them, and re-layouts: 1.63 us -> none
where the time goes in v2:
time: 146 us
  Pallas kernels  144 us (99%)
  local copies, waits for them, and re-layouts  1.98 us (1%)
    pallas_call x1, Pallas kernels, kernel_body(): pl.pallas_call(functools.partial(layer_kernel, nz, ns, span_count), out_s...  144 us

profile of v2, /device:TPU:0, one launch (start us, length us, event | category | flops | bytes accessed | tf_op | source)
XLA Modules:
  0.0 146.1 jit_solution(3751277666483338309)
XLA Ops:
  0.0 144.1 %shard_map.82 = bf16[48,3072]{1,0:T(8,128)(2,1)} custom-call(s32[16]{0:T(128)} %order_ref.1, s32[1,1536]{1,0:T(1,128)} %constant.2.clone.key_span_ref, bf16[24,2,3072]{2,1,0:T(2,128)(2,1)} %latent_ref.1, f32[6,2,3072]{2,1,0:T(2,128)} %bitcast.6, bf16[3,3072,512]{2,1,0:T(8,128)(2,1)} %qkv_hbm.1, bf16[512,3072]{1,0:T(8,128)(2,1)} %out_hbm.1, ...), custom_call_target="tpu_custom_call" | custom-call | flops 10267656192 | bytes 50331648 | tf_op jit(solution)/shard_map/pallas_call | solution.py:493
  144.1 2.0 %copy.11 = bf16[2,24,3072]{2,0,1:T(2,128)(2,1)} copy(bf16[2,24,3072]{2,1,0:T(8,128)(2,1)} %bitcast.5) | data formatting | bytes 589824 | tf_op jit(solution)/shard_map/reshape | solution.py:538

commit v3 on v2

--- a/solution.py
+++ b/solution.py
@@ -9,7 +9,7 @@
 from jax.sharding import PartitionSpec as P
 
 HD = 128
-CHUNKS = 4
+CHUNKS = 6
 BLOCK = 512
 MESH = pl.DeviceIdType.MESH
 VMEM_BYTES = 62 * 1024 * 1024
@@ -110,6 +110,9 @@
     z = lax.axis_index("space")
     me = lax.axis_index("span")
     rows, width = x_ref.shape
+    whole = pl.ds(0, rows)
+    cut = 16 * (rows // 16 - rows // 48)
+    parts = (pl.ds(0, cut), pl.ds(cut, rows - cut))
     tok = rows // span_count
     wide = width // CHUNKS
     last = nz - 1
@@ -121,7 +124,7 @@
         return pltpu.make_async_copy(src, dst, w_sem.at[slot])
 
     def columns(c, size):
-        return pl.ds(c * size, size)
+        return pl.ds(pl.multiple_of(c * size, size), size)
 
     qkv_loads = [load(qkv_hbm.at[i], w_a.at[i], i) for i in range(3)]
     out_load = load(out_hbm, w_out, 3)
@@ -167,46 +170,58 @@
     def ag_gets(way, s):
         return z - 1 - s >= 0 if way == 0 else z + 1 + s <= last
 
-    def ag_own(which, own, buf, c):
+    def ag_own(which, own, buf, c, at):
         for way in range(2):
             @pl.when(ag_sends(way, 0))
             def _():
-                ag_copy(which, way, 0, c, own.at[:, columns(c, wide)], buf.at[z, :, columns(c, wide)]).start()
-
-    def ag_step(which, buf, s, c):
+                ag_copy(
+                    which, way, 0, c, own.at[at, columns(c, wide)], buf.at[z, at, columns(c, wide)]
+                ).start()
+
+    def ag_step(which, buf, s, c, at):
         for way in range(2):
             block = z - 1 - s if way == 0 else z + 1 + s
 
             @pl.when(ag_gets(way, s))
             def _():
-                piece = buf.at[block, :, columns(c, wide)]
+                piece = buf.at[block, at, columns(c, wide)]
                 ag_copy(which, way, s, c, piece, piece).wait_recv()
 
             if s + 1 < last:
                 @pl.when(ag_sends(way, s + 1))
                 def _():
-                    piece = buf.at[block, :, columns(c, wide)]
+                    piece = buf.at[block, at, columns(c, wide)]
                     ag_copy(which, way, s + 1, c, piece, piece).start()
 
-    def ag_drain(which, buf):
-        for way in range(2):
-            for s in range(last):
-                for c in range(CHUNKS):
+    def ag_drain(which, buf, at):
+        @pl.loop(0, CHUNKS)
+        def _(c):
+            for way in range(2):
+                for s in range(last):
                     @pl.when(ag_sends(way, s))
                     def _():
-                        piece = buf.at[0, :, columns(c, wide)]
+                        piece = buf.at[0, at, columns(c, wide)]
                         ag_copy(which, way, s, c, piece, piece).wait_send()
 
-    def norm_block(block, first):
+    def segments(at):
+        first, end = at.start, at.start + at.size
+        runs = []
+        for a in range(span_count):
+            low, high = max(first, a * tok), min(end, (a + 1) * tok)
+            if low < high:
+                runs.append((a, low - first, high - first))
+        return runs
+
+    def norm_block(block, first, at):
         r = block.astype(jnp.float32)
         centred = r - jnp.mean(r, axis=-1, keepdims=True)
         variance = jnp.mean(centred * centred, axis=-1, keepdims=True)
         y = centred * lax.rsqrt(variance + 1e-06)
         pieces = []
-        for a in range(span_count):
+        for a, low, high in segments(at):
             shift = mod_ref[first, a : a + 1, :]
             scale = mod_ref[first + 1, a : a + 1, :]
-            pieces.append(y[a * tok : (a + 1) * tok] * (1.0 + scale) + shift)
+            pieces.append(y[low:high] * (1.0 + scale) + shift)
         return jnp.concatenate(pieces, axis=0).astype(jnp.bfloat16)
 
     def flip_all(index, rel):
@@ -232,7 +247,7 @@
         ).wait_recv()
 
     def project(block, source, first):
-        rows_in = norm_block(source, 0)
+        rows_in = norm_block(source, 0, whole)
 
         def part_of(i):
             if first:
@@ -271,8 +286,10 @@
                 def _():
                     do(z - 1 - s if way == 0 else z + 1 + s)
 
-    for c in range(CHUNKS):
-        ag_own(0, x_ref, gathered, c)
+    @pl.loop(0, CHUNKS)
+    def _(c):
+        ag_own(0, x_ref, gathered, c, whole)
+
     out_load.start()
     for copy in up_loads:
         copy.start()
@@ -280,8 +297,10 @@
         copy.start()
     project(z, x_ref[...], True)
     for s in range(last):
-        for c in range(CHUNKS):
-            ag_step(0, gathered, s, c)
+        @pl.loop(0, CHUNKS)
+        def _(c):
+            ag_step(0, gathered, s, c, whole)
+
         each_block(s, lambda block: project(block, gathered[block], False))
         each_block(s - 1, second_hop)
         each_block(s - 2, third_hop)
@@ -290,7 +309,7 @@
     each_block(last - 1, second_hop)
     each_block(last - 2, third_hop)
     each_block(last - 1, third_hop)
-    ag_drain(0, gathered)
+    ag_drain(0, gathered, whole)
 
     @pl.loop(0, nz)
     def _(block):
@@ -348,26 +367,32 @@
                 bit = rel & -rel if rel != 6 else (4 if which == 0 else 2)
                 kv_copy(which, rel, bit, block).wait_send()
 
-    def rs_copy(which, way, s, c, owner):
-        buf = ((from_left, from_right), (from_left2, from_right2))[which][way]
+    def rs_buf(stage, way):
+        return ((from_left, from_right), (from_left2, from_right2))[stage][way]
+
+    def rs_copy(stage, p, way, s, c, owner):
+        at = parts[p]
         return pltpu.make_async_remote_copy(
-            src_ref=part.at[owner, :, columns(c, wide)], dst_ref=buf.at[owner, :, columns(c, wide)],
-            send_sem=rs_send.at[which, way, s, c], recv_sem=rs_recv.at[which, way, s, c],
+            src_ref=part.at[owner, at, columns(c, wide)],
+            dst_ref=rs_buf(stage, way).at[owner, at, columns(c, wide)],
+            send_sem=rs_send.at[2 * stage + p, way, s, c], recv_sem=rs_recv.at[2 * stage + p, way, s, c],
             device_id=(me, z + 1 if way == 0 else z - 1), device_id_type=MESH,
         )
 
-    def rs_start(which, c):
+    def rs_start(stage, p, c):
         @pl.when(z == 0)
         def _():
             for s in range(last):
-                rs_copy(which, 0, s, c, last - s).start()
+                rs_copy(stage, p, 0, s, c, last - s).start()
 
         @pl.when(z == last)
         def _():
             for s in range(last):
-                rs_copy(which, 1, s, c, s).start()
-
-    def rs_pass(which, c):
+                rs_copy(stage, p, 1, s, c, s).start()
+
+    def rs_pass(stage, p, c):
+        at, cols = parts[p], columns(c, wide)
+        size = at.size
         for s in range(last):
             for way in range(2):
                 owner = last - s if way == 0 else s
@@ -375,101 +400,166 @@
 
                 @pl.when(on)
                 def _():
-                    copy = rs_copy(which, way, s, c, owner)
+                    copy = rs_copy(stage, p, way, s, c, owner)
                     copy.wait_recv()
-                    buf = ((from_left, from_right), (from_left2, from_right2))[which][way]
-                    at = columns(c, wide)
-                    part[owner, :, at] = (
-                        part[owner, :, at].astype(jnp.float32) + buf[owner, :, at].astype(jnp.float32)
+                    part[owner, at, cols] = (
+                        part[owner, at, cols].astype(jnp.float32)
+                        + rs_buf(stage, way)[owner, at, cols].astype(jnp.float32)
                     ).astype(jnp.bfloat16)
                     copy.start()
 
-        acc[...] = part[z, :, columns(c, wide)].astype(jnp.float32)
+        acc[0:size, :] = part[z, at, cols].astype(jnp.float32)
 
         @pl.when(z > 0)
         def _():
-            rs_copy(which, 0, last - z, c, z).wait_recv()
-            buf = (from_left, from_left2)[which]
-            acc[...] += buf[z, :, columns(c, wide)].astype(jnp.float32)
+            rs_copy(stage, p, 0, last - z, c, z).wait_recv()
+            acc[0:size, :] += rs_buf(stage, 0)[z, at, cols].astype(jnp.float32)
 
         @pl.when(z < last)
         def _():
-            rs_copy(which, 1, z, c, z).wait_recv()
-            buf = (from_right, from_right2)[which]
-            acc[...] += buf[z, :, columns(c, wide)].astype(jnp.float32)
-
-    def rs_drain(which):
-        for s in range(last):
-            for way in range(2):
-                owner = last - s if way == 0 else s
-                for c in range(CHUNKS):
+            rs_copy(stage, p, 1, z, c, z).wait_recv()
+            acc[0:size, :] += rs_buf(stage, 1)[z, at, cols].astype(jnp.float32)
+
+    def rs_drain(stage, p):
+        @pl.loop(0, CHUNKS)
+        def _(c):
+            for s in range(last):
+                for way in range(2):
+                    owner = last - s if way == 0 else s
+
                     @pl.when(owner > z if way == 0 else owner < z)
                     def _():
-                        rs_copy(which, way, s, c, owner).wait_send()
-
-    def gated(base, gate, c):
+                        rs_copy(stage, p, way, s, c, owner).wait_send()
+
+    def gated(base, gate, c, at):
+        base = base.astype(jnp.float32)
         pieces = []
-        for a in range(span_count):
-            span_rows = slice(a * tok, (a + 1) * tok)
-            factor_row = mod_ref[gate, a : a + 1, columns(c, wide)]
-            pieces.append(base[span_rows] + factor_row * acc[span_rows, :])
+        for a, low, high in segments(at):
+            row = mod_ref[gate, a : a + 1, columns(c, wide)]
+            pieces.append(base[low:high] + row * acc[low:high, :])
         return jnp.concatenate(pieces, axis=0).astype(jnp.bfloat16)
 
+    def residual_step(p, c):
+        at, cols = parts[p], columns(c, wide)
+        rs_pass(0, p, c)
+        resid[z, at, cols] = gated(x_ref[at, cols], 2, c, at)
+        ag_own(1 + p, resid.at[z], resid, c, at)
+        for s in range(last - 1):
+            @pl.when(c >= 1 + s)
+            def _():
+                ag_step(1 + p, resid, s, c - 1 - s, at)
+
+    def residual_tail(p):
+        at = parts[p]
+        for c in range(CHUNKS, CHUNKS + last - 1):
+            for s in range(last - 1):
+                if 0 <= c - 1 - s < CHUNKS:
+                    ag_step(1 + p, resid, s, c - 1 - s, at)
+
+        @pl.loop(0, CHUNKS)
+        def _(c):
+            ag_step(1 + p, resid, last - 1, c, at)
+
+    def second_norm(p):
+        at = parts[p]
+
+        @pl.loop(0, nz)
+        def _(block):
+            normed[block, at, :] = norm_block(resid[block, at, :], 3, at)
+
+    def up(p, i):
+        at = parts[p]
+        raised = jnp.dot(
+            normed[:, at, :].reshape(nz * at.size, width), w_up[i], preferred_element_type=jnp.float32
+        )
+        hidden[:, at, columns(i, BLOCK)] = (
+            jax.nn.gelu(raised, approximate=True).astype(jnp.bfloat16).reshape(nz, at.size, BLOCK)
+        )
+
+    def down(p, i, weight):
+        at = parts[p]
+        part[:, at, columns(i, BLOCK)] = (
+            jnp.dot(
+                hidden[:, at, :].reshape(nz * at.size, hidden.shape[2]),
+                weight,
+                preferred_element_type=jnp.float32,
+            )
+            .astype(jnp.bfloat16)
+            .reshape(nz, at.size, BLOCK)
+        )
+        rs_start(1, p, i)
+
+    def finish(p, c):
+        at, cols = parts[p], columns(c, wide)
+        rs_pass(1, p, c)
+        mixed_ref[at, cols] = gated(resid[z, at, cols], 5, c, at)
+
     out_load.wait()
-    for c in range(CHUNKS):
+
+    @pl.loop(0, CHUNKS)
+    def _(c):
         part[:, :, columns(c, wide)] = (
             jnp.dot(attended[...], w_out[:, columns(c, wide)], preferred_element_type=jnp.float32)
             .astype(jnp.bfloat16)
             .reshape(nz, rows, wide)
         )
-        rs_start(0, c)
-    for c in range(CHUNKS + last - 1):
-        if c < CHUNKS:
-            at = columns(c, wide)
-            rs_pass(0, c)
-            resid[z, :, at] = gated(x_ref[:, at].astype(jnp.float32), 2, c)
-            ag_own(1, resid.at[z], resid, c)
-        for s in range(last - 1):
-            if 0 <= c - 1 - s < CHUNKS:
-                ag_step(1, resid, s, c - 1 - s)
-    rs_drain(0)
-    for c in range(CHUNKS):
-        ag_step(1, resid, last - 1, c)
-
-    @pl.loop(0, nz)
-    def _(block):
-        normed[block] = norm_block(resid[block], 3)
-
+        rs_start(0, 0, c)
+
+    @pl.loop(0, CHUNKS)
+    def _(c):
+        residual_step(0, c)
+        rs_start(0, 1, c)
+
+    residual_tail(0)
+    second_norm(0)
     for copy in up_loads:
         copy.wait()
 
-    @pl.loop(0, w_up.shape[0])
+    @pl.loop(0, CHUNKS)
+    def _(c):
+        residual_step(1, c)
+        up(0, c)
+
+    for copy in down_loads:
+        copy.wait()
+    rs_drain(0, 0)
+    rs_drain(0, 1)
+
+    @pl.loop(0, first_blocks)
     def _(i):
-        raised = jnp.dot(
-            normed[...].reshape(total_rows, width), w_up[i], preferred_element_type=jnp.float32
-        )
-        hidden[:, pl.ds(pl.multiple_of(i * BLOCK, BLOCK), BLOCK)] = jax.nn.gelu(
-            raised, approximate=True
-        ).astype(jnp.bfloat16)
-
-    ag_drain(1, resid)
-    done = 0
-    for i in range(down_blocks):
-        down_loads[i].wait()
-        weight = w_b[i] if i < first_blocks else w_a[i - first_blocks]
-        part[:, :, columns(i, BLOCK)] = (
-            jnp.dot(hidden[...], weight, preferred_element_type=jnp.float32)
-            .astype(jnp.bfloat16)
-            .reshape(nz, rows, BLOCK)
-        )
-        while done < CHUNKS and (done + 1) * wide <= (i + 1) * BLOCK:
-            rs_start(1, done)
-            done += 1
-    for c in range(CHUNKS):
-        at = columns(c, wide)
-        rs_pass(1, c)
-        mixed_ref[:, at] = gated(resid[z, :, at].astype(jnp.float32), 5, c)
-    rs_drain(1)
+        down(0, i, w_b[i])
+
+    residual_tail(1)
+
+    @pl.loop(first_blocks, down_blocks)
+    def _(i):
+        down(0, i, w_a[i - first_blocks])
+
+    second_norm(1)
+    early = CHUNKS // 2
+
+    @pl.loop(0, early)
+    def _(c):
+        up(1, 2 * c)
+        up(1, 2 * c + 1)
+        finish(0, c)
+
+    @pl.loop(0, early)
+    def _(c):
+        down(1, c, w_b[c])
+        finish(0, early + c)
+
+    @pl.loop(first_blocks, down_blocks)
+    def _(i):
+        down(1, i, w_a[i - first_blocks])
+
+    @pl.loop(0, CHUNKS)
+    def _(c):
+        finish(1, c)
+
+    for p in range(2):
+        ag_drain(1 + p, resid, parts[p])
+        rs_drain(1, p)
 
 
 def kernel_body(nz, ns, latents, span_order, modulation, qkv_weight, out_weight, up_weight, down_weight):
@@ -515,16 +605,16 @@
             grouped,
             grouped,
             grouped,
-            pltpu.VMEM((total, hid), bf),
+            pltpu.VMEM((nz, rows, hid), bf),
             pltpu.VMEM((rows, width // CHUNKS), f32),
             pltpu.VMEM((1, keys_rows), jnp.int32),
             pltpu.SemaphoreType.DMA((4 + hid // BLOCK + blocks,)),
-            pltpu.SemaphoreType.DMA((2, 2, nz - 1, CHUNKS)),
-            pltpu.SemaphoreType.DMA((2, 2, nz - 1, CHUNKS)),
+            pltpu.SemaphoreType.DMA((3, 2, nz - 1, CHUNKS)),
+            pltpu.SemaphoreType.DMA((3, 2, nz - 1, CHUNKS)),
             pltpu.SemaphoreType.DMA((2, ns, nz)),
             pltpu.SemaphoreType.DMA((2, ns, nz)),
-            pltpu.SemaphoreType.DMA((2, 2, nz - 1, CHUNKS)),
-            pltpu.SemaphoreType.DMA((2, 2, nz - 1, CHUNKS)),
+            pltpu.SemaphoreType.DMA((4, 2, nz - 1, CHUNKS)),
+            pltpu.SemaphoreType.DMA((4, 2, nz - 1, CHUNKS)),
         ],
         compiler_params=pltpu.CompilerParams(
             collective_id=0, has_side_effects=True, vmem_limit_bytes=VMEM_BYTES
@@ -548,12 +638,11 @@
     return (
         ns == 8
         and nz > 1
-        and rows % 16 == 0
+        and rows % 48 == 0
         and tok % 8 == 0
         and head_cols == BLOCK
         and width == hid
-        and width % BLOCK == 0
-        and width % (CHUNKS * HD) == 0
+        and width == CHUNKS * BLOCK
         and weights + moving < VMEM_BYTES
     )
 

time: 146 us -> 232 us (1.59)
  Pallas kernels: 144 us -> 230 us
    pallas_call x1, Pallas kernels: 144 us -> 230 us  [kernel_body(): pl.pallas_call(functools.partial(layer_kernel, nz, ns, span_count), out_s...]
where the time goes in v3:
time: 232 us
  Pallas kernels  230 us (99%)
    pallas_call x1, Pallas kernels, kernel_body(): pl.pallas_call(functools.partial(layer_kernel, nz, ns, span_count), out_s...  230 us

profile of v3, /device:TPU:0, one launch (start us, length us, event | category | flops | bytes accessed | tf_op | source)
XLA Modules:
  0.0 232.0 jit_solution(15504067512515245810)
XLA Ops:
  0.0 230.0 %shard_map.82 = bf16[48,3072]{1,0:T(8,128)(2,1)} custom-call(s32[16]{0:T(128)} %order_ref.1, s32[1,1536]{1,0:T(1,128)} %constant.2.clone.key_span_ref, bf16[24,2,3072]{2,1,0:T(2,128)(2,1)} %latent_ref.1, f32[6,2,3072]{2,1,0:T(2,128)} %bitcast.6, bf16[3,3072,512]{2,1,0:T(8,128)(2,1)} %qkv_hbm.1, bf16[512,3072]{1,0:T(8,128)(2,1)} %out_hbm.1, ...), custom_call_target="tpu_custom_call" | custom-call | flops 10267656192 | bytes 50331648 | tf_op jit(solution)/shard_map/pallas_call | solution.py:583
  230.0 2.0 copy.11

commit v4 on v2

--- a/solution.py
+++ b/solution.py
@@ -9,7 +9,7 @@
 from jax.sharding import PartitionSpec as P
 
 HD = 128
-CHUNKS = 4
+CHUNKS = 6
 BLOCK = 512
 MESH = pl.DeviceIdType.MESH
 VMEM_BYTES = 62 * 1024 * 1024
@@ -110,6 +110,7 @@
     z = lax.axis_index("space")
     me = lax.axis_index("span")
     rows, width = x_ref.shape
+    whole = pl.ds(0, rows)
     tok = rows // span_count
     wide = width // CHUNKS
     last = nz - 1
@@ -121,7 +122,7 @@
         return pltpu.make_async_copy(src, dst, w_sem.at[slot])
 
     def columns(c, size):
-        return pl.ds(c * size, size)
+        return pl.ds(c * size if isinstance(c, int) else pl.multiple_of(c * size, size), size)
 
     qkv_loads = [load(qkv_hbm.at[i], w_a.at[i], i) for i in range(3)]
     out_load = load(out_hbm, w_out, 3)
@@ -167,46 +168,58 @@
     def ag_gets(way, s):
         return z - 1 - s >= 0 if way == 0 else z + 1 + s <= last
 
-    def ag_own(which, own, buf, c):
+    def ag_own(which, own, buf, c, at):
         for way in range(2):
             @pl.when(ag_sends(way, 0))
             def _():
-                ag_copy(which, way, 0, c, own.at[:, columns(c, wide)], buf.at[z, :, columns(c, wide)]).start()
-
-    def ag_step(which, buf, s, c):
+                ag_copy(
+                    which, way, 0, c, own.at[at, columns(c, wide)], buf.at[z, at, columns(c, wide)]
+                ).start()
+
+    def ag_step(which, buf, s, c, at):
         for way in range(2):
             block = z - 1 - s if way == 0 else z + 1 + s
 
             @pl.when(ag_gets(way, s))
             def _():
-                piece = buf.at[block, :, columns(c, wide)]
+                piece = buf.at[block, at, columns(c, wide)]
                 ag_copy(which, way, s, c, piece, piece).wait_recv()
 
             if s + 1 < last:
                 @pl.when(ag_sends(way, s + 1))
                 def _():
-                    piece = buf.at[block, :, columns(c, wide)]
+                    piece = buf.at[block, at, columns(c, wide)]
                     ag_copy(which, way, s + 1, c, piece, piece).start()
 
-    def ag_drain(which, buf):
-        for way in range(2):
-            for s in range(last):
-                for c in range(CHUNKS):
+    def ag_drain(which, buf, at):
+        @pl.loop(0, CHUNKS)
+        def _(c):
+            for way in range(2):
+                for s in range(last):
                     @pl.when(ag_sends(way, s))
                     def _():
-                        piece = buf.at[0, :, columns(c, wide)]
+                        piece = buf.at[0, at, columns(c, wide)]
                         ag_copy(which, way, s, c, piece, piece).wait_send()
 
-    def norm_block(block, first):
+    def segments(at):
+        first, end = at.start, at.start + at.size
+        runs = []
+        for a in range(span_count):
+            low, high = max(first, a * tok), min(end, (a + 1) * tok)
+            if low < high:
+                runs.append((a, low - first, high - first))
+        return runs
+
+    def norm_block(block, first, at):
         r = block.astype(jnp.float32)
         centred = r - jnp.mean(r, axis=-1, keepdims=True)
         variance = jnp.mean(centred * centred, axis=-1, keepdims=True)
         y = centred * lax.rsqrt(variance + 1e-06)
         pieces = []
-        for a in range(span_count):
+        for a, low, high in segments(at):
             shift = mod_ref[first, a : a + 1, :]
             scale = mod_ref[first + 1, a : a + 1, :]
-            pieces.append(y[a * tok : (a + 1) * tok] * (1.0 + scale) + shift)
+            pieces.append(y[low:high] * (1.0 + scale) + shift)
         return jnp.concatenate(pieces, axis=0).astype(jnp.bfloat16)
 
     def flip_all(index, rel):
@@ -232,7 +245,7 @@
         ).wait_recv()
 
     def project(block, source, first):
-        rows_in = norm_block(source, 0)
+        rows_in = norm_block(source, 0, whole)
 
         def part_of(i):
             if first:
@@ -243,7 +256,7 @@
             kv[which, me, block] = part_of(1 + which)
             for bit in ((2, 4, 1), (4, 2, 1))[which]:
                 kv_copy(which, bit, bit, block).start()
-        query[block] = part_of(0)
+        normed[block] = rows_in
 
     def second_hop(block):
         kv_take(0, 2, block)
@@ -271,8 +284,10 @@
                 def _():
                     do(z - 1 - s if way == 0 else z + 1 + s)
 
-    for c in range(CHUNKS):
-        ag_own(0, x_ref, gathered, c)
+    @pl.loop(0, CHUNKS)
+    def _(c):
+        ag_own(0, x_ref, gathered, c, whole)
+
     out_load.start()
     for copy in up_loads:
         copy.start()
@@ -280,17 +295,25 @@
         copy.start()
     project(z, x_ref[...], True)
     for s in range(last):
-        for c in range(CHUNKS):
-            ag_step(0, gathered, s, c)
+        @pl.loop(0, CHUNKS)
+        def _(c):
+            ag_step(0, gathered, s, c, whole)
+
         each_block(s, lambda block: project(block, gathered[block], False))
         each_block(s - 1, second_hop)
         each_block(s - 2, third_hop)
+    each_block(last - 1, second_hop)
+    qkv_loads[0].wait()
+    query[...] = (
+        jnp.dot(normed[...].reshape(nz * rows, width), w_a[0], preferred_element_type=jnp.float32)
+        .astype(jnp.bfloat16)
+        .reshape(query.shape)
+    )
     for copy in down_loads[first_blocks:]:
         copy.start()
-    each_block(last - 1, second_hop)
     each_block(last - 2, third_hop)
     each_block(last - 1, third_hop)
-    ag_drain(0, gathered)
+    ag_drain(0, gathered, whole)
 
     @pl.loop(0, nz)
     def _(block):
@@ -348,97 +371,134 @@
                 bit = rel & -rel if rel != 6 else (4 if which == 0 else 2)
                 kv_copy(which, rel, bit, block).wait_send()
 
-    def rs_copy(which, way, s, c, owner):
-        buf = ((from_left, from_right), (from_left2, from_right2))[which][way]
+    def rs_buf(stage, way):
+        return ((from_left, from_right), (from_left2, from_right2))[stage][way]
+
+    def rs_copy(stage, way, s, c, owner):
         return pltpu.make_async_remote_copy(
-            src_ref=part.at[owner, :, columns(c, wide)], dst_ref=buf.at[owner, :, columns(c, wide)],
-            send_sem=rs_send.at[which, way, s, c], recv_sem=rs_recv.at[which, way, s, c],
+            src_ref=part.at[owner, :, columns(c, wide)],
+            dst_ref=rs_buf(stage, way).at[owner, :, columns(c, wide)],
+            send_sem=rs_send.at[stage, way, s, c], recv_sem=rs_recv.at[stage, way, s, c],
             device_id=(me, z + 1 if way == 0 else z - 1), device_id_type=MESH,
         )
 
-    def rs_start(which, c):
+    def rs_start(stage, c):
         @pl.when(z == 0)
         def _():
             for s in range(last):
-                rs_copy(which, 0, s, c, last - s).start()
+                rs_copy(stage, 0, s, c, last - s).start()
 
         @pl.when(z == last)
         def _():
             for s in range(last):
-                rs_copy(which, 1, s, c, s).start()
-
-    def rs_pass(which, c):
-        for s in range(last):
-            for way in range(2):
+                rs_copy(stage, 1, s, c, s).start()
+
+    def live(c):
+        return jnp.logical_and(c >= 0, c < CHUNKS)
+
+    def farther(at):
+        return jnp.where(2 * at > last, at, last - at)
+
+    def rs_tick(stage, t, then):
+        for way in range(2):
+            c = t + 1 - z if way == 0 else t + 1 - last + z
+            inner = z > 0 if way == 0 else z < last
+            for s in range(last):
                 owner = last - s if way == 0 else s
-                on = jnp.logical_and(z > 0, owner > z) if way == 0 else jnp.logical_and(z < last, owner < z)
-
-                @pl.when(on)
+                beyond = owner > z if way == 0 else owner < z
+
+                @pl.when(jnp.logical_and(jnp.logical_and(inner, beyond), live(c)))
                 def _():
-                    copy = rs_copy(which, way, s, c, owner)
+                    cols = columns(c, wide)
+                    copy = rs_copy(stage, way, s, c, owner)
                     copy.wait_recv()
-                    buf = ((from_left, from_right), (from_left2, from_right2))[which][way]
-                    at = columns(c, wide)
-                    part[owner, :, at] = (
-                        part[owner, :, at].astype(jnp.float32) + buf[owner, :, at].astype(jnp.float32)
+                    part[owner, :, cols] = (
+                        part[owner, :, cols].astype(jnp.float32)
+                        + rs_buf(stage, way)[owner, :, cols].astype(jnp.float32)
                     ).astype(jnp.bfloat16)
                     copy.start()
 
-        acc[...] = part[z, :, columns(c, wide)].astype(jnp.float32)
-
-        @pl.when(z > 0)
+        own = t + 1 - farther(z)
+
+        @pl.when(live(own))
         def _():
-            rs_copy(which, 0, last - z, c, z).wait_recv()
-            buf = (from_left, from_left2)[which]
-            acc[...] += buf[z, :, columns(c, wide)].astype(jnp.float32)
-
-        @pl.when(z < last)
-        def _():
-            rs_copy(which, 1, z, c, z).wait_recv()
-            buf = (from_right, from_right2)[which]
-            acc[...] += buf[z, :, columns(c, wide)].astype(jnp.float32)
-
-    def rs_drain(which):
-        for s in range(last):
-            for way in range(2):
-                owner = last - s if way == 0 else s
-                for c in range(CHUNKS):
+            cols = columns(own, wide)
+            acc[...] = part[z, :, cols].astype(jnp.float32)
+
+            @pl.when(z > 0)
+            def _():
+                rs_copy(stage, 0, last - z, own, z).wait_recv()
+                acc[...] += rs_buf(stage, 0)[z, :, cols].astype(jnp.float32)
+
+            @pl.when(z < last)
+            def _():
+                rs_copy(stage, 1, z, own, z).wait_recv()
+                acc[...] += rs_buf(stage, 1)[z, :, cols].astype(jnp.float32)
+
+            then(own)
+
+    def rs_drain(stage):
+        @pl.loop(0, CHUNKS)
+        def _(c):
+            for s in range(last):
+                for way in range(2):
+                    owner = last - s if way == 0 else s
+
                     @pl.when(owner > z if way == 0 else owner < z)
                     def _():
-                        rs_copy(which, way, s, c, owner).wait_send()
+                        rs_copy(stage, way, s, c, owner).wait_send()
+
+    def ag_tick(t):
+        for way in range(2):
+            for s in range(last):
+                block = z - 1 - s if way == 0 else z + 1 + s
+                c = t - farther(block) - s
+
+                @pl.when(jnp.logical_and(ag_gets(way, s), live(c)))
+                def _():
+                    piece = resid.at[block, :, columns(c, wide)]
+                    ag_copy(1, way, s, c, piece, piece).wait_recv()
+                    if s + 1 < last:
+                        @pl.when(ag_sends(way, s + 1))
+                        def _():
+                            ag_copy(1, way, s + 1, c, piece, piece).start()
 
     def gated(base, gate, c):
+        base = base.astype(jnp.float32)
         pieces = []
-        for a in range(span_count):
-            span_rows = slice(a * tok, (a + 1) * tok)
-            factor_row = mod_ref[gate, a : a + 1, columns(c, wide)]
-            pieces.append(base[span_rows] + factor_row * acc[span_rows, :])
+        for a, low, high in segments(whole):
+            row = mod_ref[gate, a : a + 1, columns(c, wide)]
+            pieces.append(base[low:high] + row * acc[low:high, :])
         return jnp.concatenate(pieces, axis=0).astype(jnp.bfloat16)
 
+    def to_residual(c):
+        cols = columns(c, wide)
+        resid[z, :, cols] = gated(x_ref[:, cols], 2, c)
+        ag_own(1, resid.at[z], resid, c, whole)
+
+    def to_mixed(c):
+        cols = columns(c, wide)
+        mixed_ref[:, cols] = gated(resid[z, :, cols], 5, c)
+
     out_load.wait()
-    for c in range(CHUNKS):
+
+    @pl.loop(0, CHUNKS)
+    def _(c):
         part[:, :, columns(c, wide)] = (
             jnp.dot(attended[...], w_out[:, columns(c, wide)], preferred_element_type=jnp.float32)
             .astype(jnp.bfloat16)
             .reshape(nz, rows, wide)
         )
         rs_start(0, c)
-    for c in range(CHUNKS + last - 1):
-        if c < CHUNKS:
-            at = columns(c, wide)
-            rs_pass(0, c)
-            resid[z, :, at] = gated(x_ref[:, at].astype(jnp.float32), 2, c)
-            ag_own(1, resid.at[z], resid, c)
-        for s in range(last - 1):
-            if 0 <= c - 1 - s < CHUNKS:
-                ag_step(1, resid, s, c - 1 - s)
-    rs_drain(0)
-    for c in range(CHUNKS):
-        ag_step(1, resid, last - 1, c)
+
+    @pl.loop(0, CHUNKS + 2 * last - 1)
+    def _(t):
+        rs_tick(0, t, to_residual)
+        ag_tick(t)
 
     @pl.loop(0, nz)
     def _(block):
-        normed[block] = norm_block(resid[block], 3)
+        normed[block] = norm_block(resid[block], 3, whole)
 
     for copy in up_loads:
         copy.wait()
@@ -448,12 +508,10 @@
         raised = jnp.dot(
             normed[...].reshape(total_rows, width), w_up[i], preferred_element_type=jnp.float32
         )
-        hidden[:, pl.ds(pl.multiple_of(i * BLOCK, BLOCK), BLOCK)] = jax.nn.gelu(
-            raised, approximate=True
-        ).astype(jnp.bfloat16)
-
-    ag_drain(1, resid)
-    done = 0
+        hidden[:, columns(i, BLOCK)] = jax.nn.gelu(raised, approximate=True).astype(jnp.bfloat16)
+
+    ag_drain(1, resid, whole)
+    rs_drain(0)
     for i in range(down_blocks):
         down_loads[i].wait()
         weight = w_b[i] if i < first_blocks else w_a[i - first_blocks]
@@ -462,13 +520,14 @@
             .astype(jnp.bfloat16)
             .reshape(nz, rows, BLOCK)
         )
-        while done < CHUNKS and (done + 1) * wide <= (i + 1) * BLOCK:
-            rs_start(1, done)
-            done += 1
-    for c in range(CHUNKS):
-        at = columns(c, wide)
-        rs_pass(1, c)
-        mixed_ref[:, at] = gated(resid[z, :, at].astype(jnp.float32), 5, c)
+        rs_start(1, i)
+        if i > 0:
+            rs_tick(1, i - 1, to_mixed)
+
+    @pl.loop(CHUNKS - 1, CHUNKS + last - 1)
+    def _(t):
+        rs_tick(1, t, to_mixed)
+
     rs_drain(1)
 
 
@@ -552,8 +611,7 @@
         and tok % 8 == 0
         and head_cols == BLOCK
         and width == hid
-        and width % BLOCK == 0
-        and width % (CHUNKS * HD) == 0
+        and width == CHUNKS * BLOCK
         and weights + moving < VMEM_BYTES
     )
 

time: 146 us -> 123 us (0.84)
  Pallas kernels: 144 us -> 121 us
    pallas_call x1, Pallas kernels: 144 us -> 121 us  [kernel_body(): pl.pallas_call(functools.partial(layer_kernel, nz, ns, span_count), out_s...]
where the time goes in v4:
time: 123 us
  Pallas kernels  121 us (98%)
  local copies, waits for them, and re-layouts  1.98 us (2%)
    pallas_call x1, Pallas kernels, kernel_body(): pl.pallas_call(functools.partial(layer_kernel, nz, ns, span_count), out_s...  121 us

profile of v4, /device:TPU:0, one launch (start us, length us, event | category | flops | bytes accessed | tf_op | source)
XLA Modules:
  0.0 122.9 jit_solution(7951663043385100386)
XLA Ops:
  0.0 120.9 %shard_map.82 = bf16[48,3072]{1,0:T(8,128)(2,1)} custom-call(s32[16]{0:T(128)} %order_ref.1, s32[1,1536]{1,0:T(1,128)} %constant.2.clone.key_span_ref, bf16[24,2,3072]{2,1,0:T(2,128)(2,1)} %latent_ref.1, f32[6,2,3072]{2,1,0:T(2,128)} %bitcast.6, bf16[3,3072,512]{2,1,0:T(8,128)(2,1)} %qkv_hbm.1, bf16[512,3072]{1,0:T(8,128)(2,1)} %out_hbm.1, ...), custom_call_target="tpu_custom_call" | custom-call | flops 10267656192 | bytes 50331648 | tf_op jit(solution)/shard_map/pallas_call | solution.py:552
  120.9 2.0 %copy.11 = bf16[2,24,3072]{2,0,1:T(2,128)(2,1)} copy(bf16[2,24,3072]{2,1,0:T(8,128)(2,1)} %bitcast.5) | data formatting | bytes 589824 | tf_op jit(solution)/shard_map/reshape | solution.py:597

commit v5 on v4

--- a/solution.py
+++ b/solution.py
@@ -333,9 +333,9 @@
 
     def head_scores(h):
         key_order = key_order_ref[...]
-        lanes = pl.ds(pl.multiple_of(h * HD, HD), HD)
+        lanes = pl.ds(h * HD, HD)
         keys = kv[0, :, :, :, lanes].reshape(keys_rows, HD)
-        scores[...] = lax.dot_general(
+        scores[h] = lax.dot_general(
             query[:, :, lanes].reshape(total_rows, HD), keys, (((1,), (1,)), ((), ())), preferred_element_type=jnp.float32
         )
         for block in range(nz):
@@ -344,7 +344,7 @@
             for a in range(span_count):
                 at = block * rows + a * tok
                 allowed = key_order <= places[a]
-                sc = jnp.where(allowed, scores[at : at + tok, :] * factor, -1e30)
+                sc = jnp.where(allowed, scores[h, at : at + tok, :] * factor, -1e30)
                 e = jnp.exp(sc - jnp.max(sc, axis=-1, keepdims=True))
                 e = jnp.where(allowed, e, 0.0)
                 out.append(e)
@@ -352,17 +352,17 @@
             expo[h, block * rows : (block + 1) * rows, :] = jnp.concatenate(out, axis=0).astype(jnp.bfloat16)
             denom[h, block * rows : (block + 1) * rows, :] = jnp.concatenate(sums, axis=0)
 
-    @pl.loop(0, heads)
-    def _(h):
-        head_scores(h)
-
-    @pl.loop(0, heads)
-    def _(h):
-        lanes = pl.ds(pl.multiple_of(h * HD, HD), HD)
+    def head_values(h):
+        lanes = pl.ds(h * HD, HD)
         mixed_values = jnp.dot(
             expo[h], kv[1, :, :, :, lanes].reshape(keys_rows, HD), preferred_element_type=jnp.float32
         )
         attended[:, lanes] = (mixed_values / denom[h]).astype(jnp.bfloat16)
+
+    for h in range(heads):
+        head_scores(h)
+    for h in range(heads):
+        head_values(h)
 
     @pl.loop(0, nz)
     def _(block):
@@ -503,8 +503,7 @@
     for copy in up_loads:
         copy.wait()
 
-    @pl.loop(0, w_up.shape[0])
-    def _(i):
+    for i in range(w_up.shape[0]):
         raised = jnp.dot(
             normed[...].reshape(total_rows, width), w_up[i], preferred_element_type=jnp.float32
         )
@@ -565,7 +564,7 @@
             pltpu.VMEM((nz, rows, head_cols), bf),
             pltpu.VMEM((2, ns, nz, rows, head_cols), bf),
             pltpu.VMEM((heads, total, keys_rows), bf),
-            pltpu.VMEM((total, keys_rows), f32),
+            pltpu.VMEM((heads, total, keys_rows), f32),
             pltpu.VMEM((heads, total, HD), f32),
             pltpu.VMEM((total, head_cols), bf),
             grouped,
@@ -603,7 +602,7 @@
     keys_rows = ns * total
     weights = 2 * width * (4 * head_cols + 2 * hid) - 2 * width * 3 * head_cols
     moving = 2 * (9 * total * width + 2 * (keys_rows + total) * head_cols)
-    moving += 2 * total * keys_rows * (head_cols // HD + 2) + 4 * total * head_cols
+    moving += 6 * total * keys_rows * (head_cols // HD) + 4 * total * head_cols
     return (
         ns == 8
         and nz > 1

time: 123 us -> 121 us (0.984)
  Pallas kernels: 121 us -> 118 us
    pallas_call x1, Pallas kernels: 121 us -> 118 us  [kernel_body(): pl.pallas_call(functools.partial(layer_kernel, nz, ns, span_count), out_s...]
where the time goes in v5:
time: 121 us; the launch traced here: 120 us
  Pallas kernels  118 us (98%)
  local copies, waits for them, and re-layouts  1.98 us (2%)
    pallas_call x1, Pallas kernels, kernel_body(): pl.pallas_call(functools.partial(layer_kernel, nz, ns, span_count), out_s...  118 us

profile of v5, /device:TPU:0, one launch (start us, length us, event | category | flops | bytes accessed | tf_op | source)
XLA Modules:
  0.0 120.4 jit_solution(1678032654689768856)
XLA Ops:
  0.0 118.4 %shard_map.82 = bf16[48,3072]{1,0:T(8,128)(2,1)} custom-call(s32[16]{0:T(128)} %order_ref.1, s32[1,1536]{1,0:T(1,128)} %constant.2.clone.key_span_ref, bf16[24,2,3072]{2,1,0:T(2,128)(2,1)} %latent_ref.1, f32[6,2,3072]{2,1,0:T(2,128)} %bitcast.6, bf16[3,3072,512]{2,1,0:T(8,128)(2,1)} %qkv_hbm.1, bf16[512,3072]{1,0:T(8,128)(2,1)} %out_hbm.1, ...), custom_call_target="tpu_custom_call" | custom-call | flops 10267656192 | bytes 50331648 | tf_op jit(solution)/shard_map/pallas_call | solution.py:551
  118.4 2.0 %copy.11 = bf16[2,24,3072]{2,0,1:T(2,128)(2,1)} copy(bf16[2,24,3072]{2,1,0:T(8,128)(2,1)} %bitcast.5) | data formatting | bytes 589824 | tf_op jit(solution)/shard_map/reshape | solution.py:596

commit v6 on v5

--- a/solution.py
+++ b/solution.py
@@ -313,7 +313,6 @@
         copy.start()
     each_block(last - 2, third_hop)
     each_block(last - 1, third_hop)
-    ag_drain(0, gathered, whole)
 
     @pl.loop(0, nz)
     def _(block):
@@ -332,12 +331,14 @@
     key_order_ref[...] = key_order
 
     def head_scores(h):
-        key_order = key_order_ref[...]
         lanes = pl.ds(h * HD, HD)
         keys = kv[0, :, :, :, lanes].reshape(keys_rows, HD)
         scores[h] = lax.dot_general(
             query[:, :, lanes].reshape(total_rows, HD), keys, (((1,), (1,)), ((), ())), preferred_element_type=jnp.float32
         )
+
+    def head_softmax(h):
+        key_order = key_order_ref[...]
         for block in range(nz):
             out = []
             sums = []
@@ -359,17 +360,14 @@
         )
         attended[:, lanes] = (mixed_values / denom[h]).astype(jnp.bfloat16)
 
+    head_scores(0)
     for h in range(heads):
-        head_scores(h)
-    for h in range(heads):
-        head_values(h)
-
-    @pl.loop(0, nz)
-    def _(block):
-        for which in range(2):
-            for rel in range(1, 8):
-                bit = rel & -rel if rel != 6 else (4 if which == 0 else 2)
-                kv_copy(which, rel, bit, block).wait_send()
+        if h + 1 < heads:
+            head_scores(h + 1)
+        head_softmax(h)
+        if h > 0:
+            head_values(h - 1)
+    head_values(heads - 1)
 
     def rs_buf(stage, way):
         return ((from_left, from_right), (from_left2, from_right2))[stage][way]
@@ -509,7 +507,6 @@
         )
         hidden[:, columns(i, BLOCK)] = jax.nn.gelu(raised, approximate=True).astype(jnp.bfloat16)
 
-    ag_drain(1, resid, whole)
     rs_drain(0)
     for i in range(down_blocks):
         down_loads[i].wait()
@@ -528,6 +525,15 @@
         rs_tick(1, t, to_mixed)
 
     rs_drain(1)
+    ag_drain(0, gathered, whole)
+    ag_drain(1, resid, whole)
+
+    @pl.loop(0, nz)
+    def _(block):
+        for which in range(2):
+            for rel in range(1, 8):
+                bit = rel & -rel if rel != 6 else (4 if which == 0 else 2)
+                kv_copy(which, rel, bit, block).wait_send()
 
 
 def kernel_body(nz, ns, latents, span_order, modulation, qkv_weight, out_weight, up_weight, down_weight):

time: 121 us -> 121 us (level)
  no operation moved by 1% of the time
where the time goes in v6:
time: 121 us
  Pallas kernels  119 us (98%)
  local copies, waits for them, and re-layouts  1.98 us (2%)
    pallas_call x1, Pallas kernels, kernel_body(): pl.pallas_call(functools.partial(layer_kernel, nz, ns, span_count), out_s...  119 us

profile of v6, /device:TPU:0, one launch (start us, length us, event | category | flops | bytes accessed | tf_op | source)
XLA Modules:
  0.0 120.5 jit_solution(2032975797865323595)
XLA Ops:
  0.0 118.5 %shard_map.82 = bf16[48,3072]{1,0:T(8,128)(2,1)} custom-call(s32[16]{0:T(128)} %order_ref.1, s32[1,1536]{1,0:T(1,128)} %constant.2.clone.key_span_ref, bf16[24,2,3072]{2,1,0:T(2,128)(2,1)} %latent_ref.1, f32[6,2,3072]{2,1,0:T(2,128)} %bitcast.6, bf16[3,3072,512]{2,1,0:T(8,128)(2,1)} %qkv_hbm.1, bf16[512,3072]{1,0:T(8,128)(2,1)} %out_hbm.1, ...), custom_call_target="tpu_custom_call" | custom-call | flops 10267656192 | bytes 50331648 | tf_op jit(solution)/shard_map/pallas_call | solution.py:557
  118.5 2.0 %copy.11 = bf16[2,24,3072]{2,0,1:T(2,128)(2,1)} copy(bf16[2,24,3072]{2,1,0:T(8,128)(2,1)} %bitcast.5) | data formatting | bytes 589824 | tf_op jit(solution)/shard_map/reshape | solution.py:602
